TPU v7x, 256 devices: a whole 4x4x8 slice. The times are simulated.
256 devices in a mesh: ctx: 32 (over z, y), head: 8 (over x, core).
Axes of the slice: x: 4, y: 4, z: 8, core: 2. Of those that a mesh axis runs over, the one named last changes fastest.
Arguments:
- x_in: bfloat16 [49152, 8192], P('ctx', 'head'), may hold values from -6 to 6
- gate_z: bfloat16 [49152, 8192], P('ctx', 'head'), may hold values from -6 to 6
- bc_in: bfloat16 [49152, 8, 256], P('ctx', 'head'), may hold values from -6 to 6
- dt_raw: float32 [49152, 128], P('ctx', 'head'), may hold values from -4 to 4
- conv_x: float32 [4, 8192], P(None, 'head'), may hold values from -3 to 3
- conv_bc: float32 [4, 8, 256], P(None, 'head'), may hold values from -3 to 3
- dt_bias: float32 [128], P('head'), may hold values from -11 to -1
- a_log: float32 [128], P('head'), may hold values from -3 to 1
- d_skip: float32 [128], P('head'), may hold values from 0.5 to 2
- norm_gain: float32 [8192], P('head'), may hold values from 0.5 to 1.5
- readout: bfloat16 [8192], P('head'), may hold values from -0.0625 to 0.0625
- lengths: int32 [16], replicated, may hold values from 1 to 24576, 49152 in all
Outputs:
- mixed_out: bfloat16 [49152, 8192], P('ctx', 'head')
- cand_scores: float32 [16], replicated
Inputs may be any that keep to these rules, and one draw needn't show every extreme that they name: `lengths`: candidate token counts; they sum to 49152, and one candidate has exactly 24576 tokens.
All inputs are finite; a program needn't handle non-finite values.
Results may differ from a plain program's by a relative error of at most 0.009.
Values may be sent and summed in bfloat16 or wider, within the bound.
A program may use at most 128 MiB of HBM per device.

v0:
```python
import jax
import jax.numpy as jnp
from jax import lax
from jax.sharding import PartitionSpec as P

STRETCH = 256


HIGHEST_PREC = lax.Precision.HIGHEST


def shifted(value, axis, steps):
    count = lax.axis_size(axis)
    initial, last = (max(0, -steps), min(count, count - steps))
    return lax.ppermute(value, axis, [(source, source + steps) for source in range(initial, last)])


def prefix(x, axis, combine, identity):
    count, mine = (lax.axis_size(axis), lax.axis_index(axis))
    everything = jax.tree.map(lambda part: lax.all_gather(part, axis), x)
    start = jax.tree.map(
        lambda part, zero: jnp.broadcast_to(jnp.asarray(zero, part.dtype), part.shape), x, identity
    )

    def lap(k, before):
        reached = k < mine
        new = combine(before, jax.tree.map(lambda part: part[k], everything))
        return jax.tree.map(lambda a, b: jnp.where(reached, a, b), new, before)

    return lax.fori_loop(0, count, lap, start)


def segment_of(positions, lengths):
    offsets = jnp.cumsum(lengths) - lengths
    return jnp.sum((positions[:, None] >= offsets[None, :]).astype(jnp.int32), axis=1) - 1


def causal_conv(extended, weights, seg_ext):
    span_count = seg_ext.shape[0] - 3
    seg_now = seg_ext[3:]
    conv_sum = jnp.zeros((span_count, extended.shape[1]), jnp.float32)
    for lag_index in range(4):
        same_doc = (seg_ext[3 - lag_index : 3 - lag_index + span_count] == seg_now).astype(
            jnp.float32
        )
        piece_in = extended[3 - lag_index : 3 - lag_index + span_count].astype(jnp.float32)
        conv_sum = conv_sum + weights[lag_index][None, :] * piece_in * same_doc[:, None]
    return jax.nn.silu(conv_sum)


def block_ssd(x_flat, bc_blk, dt_vals, decay_log, segment, seg_before, ssd_state, d_skip):
    row_count = x_flat.shape[0]
    head_count, head_dim, state_size = ssd_state.shape
    groups = bc_blk.shape[1] // (2 * state_size)
    per_group = head_count // groups
    x_conv = x_flat.reshape(row_count, head_count, head_dim)
    bc_grouped = bc_blk.reshape(row_count, groups, 2 * state_size)
    b_mat = bc_grouped[:, :, :state_size]
    c_mat = bc_grouped[:, :, state_size:]
    cumulative = jnp.cumsum(decay_log, axis=0)
    cb_scores = jnp.einsum("tgn,sgn->gts", c_mat, b_mat, precision=HIGHEST_PREC)
    cb_scores = jnp.repeat(cb_scores, per_group, axis=0)
    order_row = jnp.arange(row_count)
    inside = (segment[:, None] == segment[None, :]) & (order_row[:, None] >= order_row[None, :])
    gap_log = cumulative.T[:, :, None] - cumulative.T[:, None, :]
    weights_mat = (
        jnp.exp(jnp.where(inside[None], gap_log, -jnp.inf)) * cb_scores * dt_vals.T[:, None, :]
    )
    within = jnp.einsum("hts,shp->thp", weights_mat, x_conv, precision=HIGHEST_PREC)
    c_head = jnp.repeat(c_mat, per_group, axis=1)
    b_head = jnp.repeat(b_mat, per_group, axis=1)
    alive_mask = (segment == seg_before).astype(jnp.float32)
    carried = jnp.einsum("thn,hpn->thp", c_head, ssd_state, precision=HIGHEST_PREC)
    carried = carried * (jnp.exp(cumulative) * alive_mask[:, None])[:, :, None]
    result_y = within + carried + d_skip[None, :, None] * x_conv
    tail_weight = (
        jnp.exp(cumulative[-1][None, :] - cumulative)
        * (segment == segment[-1]).astype(jnp.float32)[:, None]
        * dt_vals
    )
    fresh_state = jnp.einsum(
        "shp,shn->hpn", tail_weight[:, :, None] * x_conv, b_head, precision=HIGHEST_PREC
    )
    new_state = fresh_state + (jnp.exp(cumulative[-1]) * alive_mask[-1])[:, None, None] * ssd_state
    return (result_y.reshape(row_count, head_count * head_dim), new_state)


def gated_norm(values, gate_in, gain_vec, groups):
    gated = values * jax.nn.silu(gate_in.astype(jnp.float32))
    grouped = gated.reshape(gated.shape[0], groups, -1)
    inv_scale = lax.rsqrt(jnp.mean(grouped * grouped, axis=2, keepdims=True) + 1e-05)
    return ((grouped * inv_scale).reshape(gated.shape) * gain_vec[None, :]).astype(jnp.bfloat16)


def chain_link(earlier, later_pair):
    return (earlier[0] * later_pair[0], later_pair[0][:, None, None] * earlier[1] + later_pair[1])


def local(
    x_in,
    gate_z,
    bc_in,
    dt_raw,
    conv_x,
    conv_bc,
    dt_bias,
    a_log,
    d_skip,
    norm_gain,
    readout,
    lengths,
):
    row_count, inner_width = x_in.shape
    head_count = dt_raw.shape[1]
    groups = bc_in.shape[1]
    state_size = bc_in.shape[2] // 2
    head_dim = inner_width // head_count
    per_group = head_count // groups
    bc_width = groups * 2 * state_size
    block_count = row_count // STRETCH
    dev_start = lax.axis_index("ctx") * row_count
    ext_positions = dev_start - 3 + jnp.arange(row_count + 3, dtype=jnp.int32)
    seg_ext = segment_of(ext_positions, lengths)
    segment = seg_ext[3:]
    seg_dev_before = seg_ext[2]
    bc_rows = bc_in.reshape(row_count, bc_width)
    tail_x, tail_bc = shifted((x_in[-3:], bc_rows[-3:]), "ctx", 1)
    x_conv = causal_conv(jnp.concatenate([tail_x, x_in]), conv_x, seg_ext)
    bc_conv = causal_conv(
        jnp.concatenate([tail_bc, bc_rows]), conv_bc.reshape(4, bc_width), seg_ext
    )
    dt_vals = jax.nn.softplus(dt_raw + dt_bias[None, :])
    decay_log = -dt_vals * jnp.exp(a_log)[None, :]

    def block_step(carry_in, block_in):
        ssd_state, seg_before = carry_in
        x_blk, bc_blk, dt_blk, dl_blk, seg_blk = block_in
        result_y, ssd_state = block_ssd(
            x_blk, bc_blk, dt_blk, dl_blk, seg_blk, seg_before, ssd_state, d_skip
        )
        return ((ssd_state, seg_blk[-1]), result_y)

    blocks_in = (
        x_conv.reshape(block_count, STRETCH, inner_width),
        bc_conv.reshape(block_count, STRETCH, bc_width),
        dt_vals.reshape(block_count, STRETCH, head_count),
        decay_log.reshape(block_count, STRETCH, head_count),
        segment.reshape(block_count, STRETCH),
    )
    carry_start = (jnp.zeros((head_count, head_dim, state_size), jnp.float32), seg_dev_before)
    (state_dev, _), y_blocks = lax.scan(block_step, carry_start, blocks_in)
    result_y = y_blocks.reshape(row_count, inner_width)
    cum_dev = jnp.cumsum(decay_log, axis=0)
    alive_dev = (segment == seg_dev_before).astype(jnp.float32)
    decay_dev = jnp.exp(cum_dev[-1]) * alive_dev[-1]
    identity = (jnp.ones_like(decay_dev), jnp.zeros_like(state_dev))
    _, inbound = prefix((decay_dev, state_dev), "ctx", chain_link, identity)
    c_mat = bc_conv.reshape(row_count, groups, 2 * state_size)[:, :, state_size:]
    c_head = jnp.repeat(c_mat, per_group, axis=1)
    entering = jnp.einsum("thn,hpn->thp", c_head, inbound, precision=HIGHEST_PREC)
    entering = entering * (jnp.exp(cum_dev) * alive_dev[:, None])[:, :, None]
    result_y = result_y + entering.reshape(row_count, inner_width)
    mixed_out = gated_norm(result_y, gate_z, norm_gain, groups)
    positions = ext_positions[3:]
    cand_ends = jnp.cumsum(lengths) - 1
    onehot = (positions[:, None] == cand_ends[None, :]).astype(jnp.float32)
    token_score = jnp.dot(mixed_out, readout, preferred_element_type=jnp.float32)
    partial_sum = jnp.dot(token_score, onehot, precision=HIGHEST_PREC)
    cand_scores = lax.psum(partial_sum, ("ctx", "head"))
    return (mixed_out, cand_scores)


def solution(mesh):
    in_specs = (
        P("ctx", "head"),
        P("ctx", "head"),
        P("ctx", "head", None),
        P("ctx", "head"),
        P(None, "head"),
        P(None, "head", None),
        P("head"),
        P("head"),
        P("head"),
        P("head"),
        P("head"),
        P(),
    )
    out_specs = (P("ctx", "head"), P())
    return jax.shard_map(local, mesh=mesh, in_specs=in_specs, out_specs=out_specs, check_vma=False)
```

profile of v0, /device:TPU:1, one launch (start us, length us, event | category | flops | bytes accessed | tf_op | source)
XLA Modules:
  0.0 444.0 jit_solution(14759344708326584838)
XLA Ops:
  7.9 4.0 collective-permute-start.1
  12.7 3.2 collective-permute-start
  22.9 4.4 divide_multiply_fusion.1
  27.4 12.0 %divide_multiply_fusion = f32[1536,1024]{1,0:T(8,128)} fusion(bf16[1536,1024]{1,0:T(8,128)(2,1)} %param.16, bf16[3,1024]{1,0:T(4,128)(2,1)S(1)} %collective-permute-done, f32[1536]{0:T(1024)S(1)} %get-tuple-element.305, f32[1024]{0:T(1024)S(1)} %bitcast.171, f32[1536]{0:T(1024)S(1)} %get-tuple-element.306, f32[1024]{0:T(1024)S(1)} %bitcast.172, ...), kind=kLoop, calls=%fused_computation.66 | loop fusion | flops 42467328 | bytes 9478144 | tf_op jit(solution)/shard_map/jit(silu)/mul | solution.py:48
  39.3 108.7 %while.29 = (s32[]{:T(128)}, f32[16,64,128]{2,1,0:T(8,128)S(1)}, s32[]{:T(128)}, f32[6,256,1024]{2,1,0:T(8,128)}, f32[6,256,16]{1,0,2:T(8,128)}, /*index=5*/s32[...) while((s32[]{:T(128)}, f32[16,64,128]{2,1,0:T(8,128)S(1)}, ...), condition=%wide.region_5.6_spmd.clone, body=%wide.region_2.5_spmd.clone.sunk | while | flops 1718047744 | bytes 18835176 | solution.py:151
  46.0 1.3 constant_dynamic-slice_fusion.7
  47.7 4.8 %fusion.78 = f32[256,16,64]{0,2,1:T(8,128)S(1)} fusion(f32[256,16,64]{0,2,1:T(8,128)S(1)} %bitcast.155, f32[16,256]{1,0:T(8,128)S(1)} %bitcast.165, f32[256,256]{1,0:T(8,128)S(1)} %fusion.76, f32[16,256]{1,0:T(8,128)S(1)} %get-tuple-element.417, pred[256,256]{1,0:T(8,128)(4,1)S(1)} %fusion.77), kind=kOutput, calls=%fused_computation.15.clone.1 | convolution fusion | flops 809500672 | bytes 2457600 | tf_op jit(solution)/shard_map/while/body/eval_jaxpr/hts,shp->thp/dot_general | solution.py:69
  52.4 2.3 fusion.79
  64.1 1.3 constant_dynamic-slice_fusion.7
  65.8 4.8 %fusion.78 = f32[256,16,64]{0,2,1:T(8,128)S(1)} fusion(f32[256,16,64]{0,2,1:T(8,128)S(1)} %bitcast.155, f32[16,256]{1,0:T(8,128)S(1)} %bitcast.165, f32[256,256]{1,0:T(8,128)S(1)} %fusion.76, f32[16,256]{1,0:T(8,128)S(1)} %get-tuple-element.417, pred[256,256]{1,0:T(8,128)(4,1)S(1)} %fusion.77), kind=kOutput, calls=%fused_computation.15.clone.1 | convolution fusion | flops 809500672 | bytes 2457600 | tf_op jit(solution)/shard_map/while/body/eval_jaxpr/hts,shp->thp/dot_general | solution.py:69
  70.6 2.3 fusion.79
  82.3 1.3 constant_dynamic-slice_fusion.7
  83.9 4.8 %fusion.78 = f32[256,16,64]{0,2,1:T(8,128)S(1)} fusion(f32[256,16,64]{0,2,1:T(8,128)S(1)} %bitcast.155, f32[16,256]{1,0:T(8,128)S(1)} %bitcast.165, f32[256,256]{1,0:T(8,128)S(1)} %fusion.76, f32[16,256]{1,0:T(8,128)S(1)} %get-tuple-element.417, pred[256,256]{1,0:T(8,128)(4,1)S(1)} %fusion.77), kind=kOutput, calls=%fused_computation.15.clone.1 | convolution fusion | flops 809500672 | bytes 2457600 | tf_op jit(solution)/shard_map/while/body/eval_jaxpr/hts,shp->thp/dot_general | solution.py:69
  88.7 2.3 fusion.79
  100.4 1.3 constant_dynamic-slice_fusion.7
  102.0 4.8 %fusion.78 = f32[256,16,64]{0,2,1:T(8,128)S(1)} fusion(f32[256,16,64]{0,2,1:T(8,128)S(1)} %bitcast.155, f32[16,256]{1,0:T(8,128)S(1)} %bitcast.165, f32[256,256]{1,0:T(8,128)S(1)} %fusion.76, f32[16,256]{1,0:T(8,128)S(1)} %get-tuple-element.417, pred[256,256]{1,0:T(8,128)(4,1)S(1)} %fusion.77), kind=kOutput, calls=%fused_computation.15.clone.1 | convolution fusion | flops 809500672 | bytes 2457600 | tf_op jit(solution)/shard_map/while/body/eval_jaxpr/hts,shp->thp/dot_general | solution.py:69
  106.8 2.3 fusion.79
  118.5 1.3 constant_dynamic-slice_fusion.7
  120.1 4.8 %fusion.78 = f32[256,16,64]{0,2,1:T(8,128)S(1)} fusion(f32[256,16,64]{0,2,1:T(8,128)S(1)} %bitcast.155, f32[16,256]{1,0:T(8,128)S(1)} %bitcast.165, f32[256,256]{1,0:T(8,128)S(1)} %fusion.76, f32[16,256]{1,0:T(8,128)S(1)} %get-tuple-element.417, pred[256,256]{1,0:T(8,128)(4,1)S(1)} %fusion.77), kind=kOutput, calls=%fused_computation.15.clone.1 | convolution fusion | flops 809500672 | bytes 2457600 | tf_op jit(solution)/shard_map/while/body/eval_jaxpr/hts,shp->thp/dot_general | solution.py:69
  124.9 2.3 fusion.79
  136.6 1.3 constant_dynamic-slice_fusion.7
  138.2 4.8 %fusion.78 = f32[256,16,64]{0,2,1:T(8,128)S(1)} fusion(f32[256,16,64]{0,2,1:T(8,128)S(1)} %bitcast.155, f32[16,256]{1,0:T(8,128)S(1)} %bitcast.165, f32[256,256]{1,0:T(8,128)S(1)} %fusion.76, f32[16,256]{1,0:T(8,128)S(1)} %get-tuple-element.417, pred[256,256]{1,0:T(8,128)(4,1)S(1)} %fusion.77), kind=kOutput, calls=%fused_computation.15.clone.1 | convolution fusion | flops 809500672 | bytes 2457600 | tf_op jit(solution)/shard_map/while/body/eval_jaxpr/hts,shp->thp/dot_general | solution.py:69
  143.0 2.3 fusion.79
  149.6 4.5 %reduce-window.23 = f32[16,12,128]{2,1,0:T(8,128)S(1)} reduce-window(f32[16,12,128]{2,1,0:T(8,128)S(1)} %reshape.243, f32[]{:T(128)} %constant.79.clone.1), window={size=1x1x128 pad=0_0x0_0x127_0}, to_apply=%region_6.7 | reduce-window | flops 3121152 | bytes 196612 | tf_op jit(solution)/shard_map/reduce-window.3
  155.6 36.6 %all-gather.1 = f32[32,1,16]{2,1,0:T(1,128)S(1)} all-gather(f32[1,1,16]{2,1,0:T(1,128)S(1)} %bitcast.178), channel_id=1, replica_groups=mesh['ctx'=32,'head'=8] {'ctx'}, dimensions={0}, use_global_device_ids=true | all-gather | bytes 2112 | tf_op jit(solution)/shard_map/all_gather | solution.py:20
  193.4 98.0 %all-gather.4.cloned.1.call-done = f32[512,64,128]{2,1,0:T(8,128)} async-done(((f32[16,64,128]{2,1,0:T(8,128)}), f32[512,64,128]{2,1,0:T(8,128)}) %all-gather.4.cloned.1.call-update) | async-done | bytes 16777232 | tf_op jit(solution)/shard_map/all_gather | solution.py:20
  291.4 39.0 %while.30 = (s32[]{:T(128)}, f32[16,64,128]{2,1,0:T(8,128)S(1)}, s32[]{:T(128)}, f32[32,16]{1,0:T(8,128)S(1)}, f32[32,16,64,128]{3,2,1,0:T(8,128)}, /*index=5*/s32[]{:T(128)}, s32[]{:T(128)}) while((s32[]{:T(128)}, f32[16,64,128]{2,1,0:T(8,128)S(1)}, s32[]{:T(128)}, f32[32,16]{1,0:T(8,128)S(1)}, f32[32,16,64,128]{3,2,1,0:T(8,128)}, ...), condition=%wide.region_9.10_spmd.clone, body=%wide.region_8.9_spmd.clone.sunk | while | flops 524292 | bytes 1573169 | solution.py:30
  330.4 14.9 %bitcast_multiply_fusion.1 = f32[1536,16,64]{0,2,1:T(8,128)} fusion(f32[16,64,128]{2,1,0:T(8,128)S(1)} %get-tuple-element.151, f32[1536,128]{1,0:T(8,128)S(1)} %slice_bitcast_fusion.4, f32[1536,16]{0,1:T(8,128)S(1)} %get-tuple-element.285), kind=kOutput, calls=%fused_computation.60 | convolution fusion | flops 2417491968 | bytes 7700480 | tf_op jit(solution)/shard_map/thn,hpn->thp/dot_general | solution.py:160
  345.2 6.6 %copy.56 = f32[1536,1024]{1,0:T(8,128)} copy(f32[1536,1024]{0,1:T(8,128)} %bitcast.159) | data formatting | bytes 12582912 | tf_op jit(solution)/shard_map/reshape | solution.py:162
  351.8 6.7 %multiply_reduce_fusion = (f32[1536]{0:T(1024)S(1)}, f32[1536,1024]{1,0:T(8,128)S(1)}) fusion(bf16[1536,1024]{1,0:T(8,128)(2,1)} %param.17, f32[1536,1024]{1,0:T(8,128)} %copy.56, f32[6,256,1024]{2,1,0:T(8,128)} %get-tuple-element.149), kind=kLoop, calls=%fused_computation.63 | loop fusion | flops 14154240 | bytes 22026240 | tf_op jit(solution)/shard_map/reduce_sum | solution.py:91
  359.2 1.7 copy-done.1
  362.2 74.9 %psum.7 = f32[16]{0:T(128)} all-reduce(f32[16]{0:T(128)S(1)} %convolution_bitcast_fusion.2), channel_id=1, replica_groups=mesh['ctx'=32,'head'=8] {'ctx','head'}, use_global_device_ids=true, to_apply=%region_11.12 | all-reduce | flops 16 | bytes 128 | tf_op jit(solution)/shard_map/psum | solution.py:169
  (251 shorter events, 106.6 us)
Async XLA Ops:
  7.2 284.2 %all-gather.4.cloned.1.call-start = ((), (), s32[]{:S(2)}) async-start(), calls=%async_computation | async-start | bytes 17301504 | tf_op jit(solution)/shard_map/all_gather | solution.py:20
  7.9 15.0 %collective-permute-start.1 = (bf16[3,256]{1,0:T(4,128)(2,1)S(1)}, bf16[3,256]{1,0:T(4,128)(2,1)S(1)}, u32[]{:S(2)}, u32[]{:S(2)}) collective-permute-start(bf16[3,256]{1,0:T(4,128)(2,1)S(1)} %slice_bitcast_fusion.5), channel_id=1, source_target_pairs={{0,8},{8,16},{16,24},{24,32},{32,40},{40,48},{48,56},{56,64},{64,7... | collective-permute-start | bytes 4616 | tf_op jit(solution)/shard_map/ppermute | solution.py:15
  12.7 14.7 %collective-permute-start = (bf16[3,1024]{1,0:T(4,128)(2,1)S(1)}, bf16[3,1024]{1,0:T(4,128)(2,1)S(1)}, u32[]{:S(2)}, u32[]{:S(2)}) collective-permute-start(bf16[3,1024]{1,0:T(4,128)(2,1)S(1)} %slice.127), channel_id=1, source_target_pairs={{0,8},{8,16},{16,24},{24,32},{32,40},{40,48},{48,56},{56,64},{64,7... | collective-permute-start | bytes 18440 | tf_op jit(solution)/shard_map/ppermute | solution.py:15
  20.4 18.9 %copy-start.2 = (f32[16]{0:T(128)S(1)}, f32[16]{0:T(128)}, u32[]{:S(2)}) copy-start(f32[16]{0:T(128)} %param.24) | copy-start | bytes 196
  39.3 109.6 %copy-start.4 = (bf16[1024]{0:T(1024)(128)(2,1)S(1)}, bf16[1024]{0:T(1024)(128)(2,1)}, u32[]{:S(2)}) copy-start(bf16[1024]{0:T(1024)(128)(2,1)} %param.26) | copy-start | bytes 6148
  148.0 0.8 copy-start
  351.8 6.7 %copy-start.3 = (f32[1024]{0:T(1024)S(1)}, f32[1024]{0:T(1024)}, u32[]{:S(2)}) copy-start(f32[1024]{0:T(1024)} %param.25) | copy-start | bytes 12292
  359.2 1.7 copy-start.1
Sparse Core Ops, SparseCore 0:
  149.0 142.3 all-gather.3
where the time goes:
time: 447 us; the launch traced here: 444 us
  blocking collectives  112 us (25%)
  waiting for transfers between devices  98 us (22%)
  other arithmetic  82.4 us (18%)
  matrix products  68.8 us (15%)
  local copies, waits for them, and re-layouts  56.3 us (13%)
  between operations  14.2 us (3%)
  starting transfers between devices  7.25 us (2%)
  loops' own time  5.55 us (1%)
    all_gather x1, waiting for transfers between devices, prefix(): everything = jax.tree.map(lambda part: lax.all_gather(part, axis), x)  98 us
    psum x1, blocking collectives, local(): cand_scores = lax.psum(partial_sum, ('ctx', 'head'))  74.9 us
    select_n x32, other arithmetic, lap(): return jax.tree.map(lambda a, b: jnp.where(reached, a, b), new, before)  37.7 us
    all_gather x1, blocking collectives, prefix(): everything = jax.tree.map(lambda part: lax.all_gather(part, axis), x)  36.6 us
    dot_general x6, matrix products, block_ssd(): jnp.einsum('hts,shp->thp', weights_mat, x_conv, precision=HIGHEST_PREC)  28.7 us
    mul x2, other arithmetic, causal_conv(): return jax.nn.silu(conv_sum)  16.4 us
    dynamic_slice x30, local copies, waits for them, and re-layouts, local(): (state_dev, _), y_blocks = lax.scan(block_step, carry_start, blocks_in)  15.5 us
    dot_general x1, matrix products, local(): jnp.einsum('thn,hpn->thp', c_head, inbound, precision=HIGHEST_PREC)  14.9 us
  transfers between devices with their start and end apart: 3, of which 1 were waited for; matrix products, arithmetic and copies ran while one was open for 5% of the time, Pallas kernels for 0%

commit v1 on v0

v1 whole, which is shorter than its diff:
```python
import functools

import jax
import jax.numpy as jnp
from jax import lax
from jax.experimental import pallas as pl
from jax.experimental.pallas import tpu as pltpu
from jax.sharding import PartitionSpec as P

F32, BF16, I32 = jnp.float32, jnp.bfloat16, jnp.int32
MESH = pl.DeviceIdType.MESH
LOG2E = 1.4426950408889634
Q = 128
QW = 256
HALO = 16
RESET = 200.0
LANES = 128
CHUNK_ROWS = 16


def iota(shape, dim):
    return lax.broadcasted_iota(I32, shape, dim)


def dot(a, b):
    return jnp.dot(a, b, preferred_element_type=F32)


def three(x):
    hi = x.astype(BF16)
    rest = x - hi.astype(F32)
    mid = rest.astype(BF16)
    return hi, mid, (rest - mid.astype(F32)).astype(BF16)


def softplus(v):
    u = jnp.exp(-jnp.abs(v))
    small = u * (1.0 + u * (-0.5 + u * (1.0 / 3.0 - 0.25 * u)))
    return jnp.maximum(v, 0.0) + jnp.where(u < 0.01, small, jnp.log(1.0 + u))


def twice_silu_half(h):
    return h + h * jnp.tanh(h)


def conv_block(rows, before, taps, shift, near):
    width = rows.shape[1]
    scaled = jnp.concatenate([rows * tap.astype(BF16) for tap in taps], axis=0)
    out = dot(shift, scaled)
    tail = before.astype(F32)[8:16]
    row = iota((8, width), 0)
    first = jnp.zeros((8, width), F32)
    near = jnp.concatenate([near] * (width // LANES), axis=1)
    for lag in (1, 2, 3):
        first = first + jnp.where(
            (row < lag) & (near >= lag), pltpu.roll(tail, lag, 0) * taps[lag], 0.0
        )
    return jnp.concatenate([out[:8] + first, out[8:]], axis=0)


def kernel(
    dims,
    lengths, bias, a_log, d_skip,
    dt_ref, conv_x, conv_bc, gain, readout, x_hbm, z_hbm, bc_hbm,
    out_hbm, score_ref,
    xq, bcs, zq, hx, hbc, shift, pos8, cols, colf, vrow, tots, dec_blk, dec_pre, sel_w, sel_e,
    xc, cmat, btr, cb, sk, state, sbuf, ypre, gated, stage, score_acc,
    my_dec, got_dec, got_s, ret_s, inbound, sc_mine, sc_ctx, got_h, got_c,
    sem_x, sem_bc, sem_z, sem_out, sem_halo_s, sem_halo_r, sem_s, sem_r,
):
    n_ctx, n_head, rows_all, heads, split = dims
    blocks = rows_all // Q
    quads = heads * 64 // QW
    pairs = heads // 2
    many = n_ctx > 1
    me = lax.axis_index("ctx")
    me_head = lax.axis_index("head")
    part_rows = Q // 4
    plane, lane_y = me // 4, me % 4

    if many:
        barrier = pltpu.get_barrier_semaphore()

        def greet_ctx(i, _):
            pl.semaphore_signal(barrier, inc=1, device_id={"ctx": lax.rem(me + i, n_ctx)}, device_id_type=MESH)
            return 0

        lax.fori_loop(1, n_ctx, greet_ctx, 0)

        def greet_head(i, _):
            pl.semaphore_signal(barrier, inc=1, device_id={"head": lax.rem(me_head + i, n_head)}, device_id_type=MESH)
            return 0

        lax.fori_loop(1, n_head, greet_head, 0)

    load_bc = pltpu.make_async_copy(bc_hbm, bcs, sem_bc)
    load_bc.start()
    load_x = [
        pltpu.make_async_copy(x_hbm.at[:, pl.ds(q * QW, QW)], xq.at[q], sem_x.at[q])
        for q in range(quads)
    ]
    load_z = [
        pltpu.make_async_copy(z_hbm.at[:, pl.ds(q * QW, QW)], zq.at[q], sem_z.at[q])
        for q in range(quads)
    ]
    for copy in load_x:
        copy.start()
    for copy in load_z:
        copy.start()

    offset = jnp.int32(0)
    here = me * rows_all + iota((CHUNK_ROWS, LANES), 0) * Q + iota((CHUNK_ROWS, LANES), 1)
    since = jnp.full((CHUNK_ROWS, LANES), 1 << 20, I32)
    ends = jnp.zeros((CHUNK_ROWS, LANES), I32)
    for c in range(lengths.shape[0]):
        gone = here - offset
        since = jnp.where(gone >= 0, jnp.minimum(since, gone), since)
        offset = offset + lengths[c]
        ends = jnp.where(iota((CHUNK_ROWS, LANES), 0) == c, offset - 1, ends)
    since = since.astype(F32)
    near = jnp.minimum(since, 3.0)

    head_row = iota((heads, LANES), 0)
    bias_col = jnp.zeros((heads, LANES), F32)
    rate_col = jnp.zeros((heads, LANES), F32)
    for h in range(heads):
        bias_col = jnp.where(head_row == h, bias[h], bias_col)
        rate_col = jnp.where(head_row == h, a_log[h], rate_col)
    rate_col = jnp.exp(rate_col) * (-LOG2E)
    steps, logs = [], []
    for k in range(blocks):
        dt_vals = softplus(dt_ref[:, k * Q : (k + 1) * Q] + bias_col)
        steps.append(jnp.log(dt_vals) * LOG2E)
        fresh = jnp.where(since[k : k + 1] == 0.0, RESET, 0.0)
        logs.append(dt_vals * rate_col - fresh)
    upper = (iota((Q, Q), 0) <= iota((Q, Q), 1)).astype(F32).astype(BF16)
    cum_all = dot(
        jnp.concatenate(three(jnp.concatenate(logs, axis=0)), axis=1),
        jnp.concatenate([upper] * 3, axis=0),
    )
    before = jnp.zeros((heads, LANES), F32)
    for k in range(blocks):
        cum = cum_all[k * heads : (k + 1) * heads]
        value = steps[k] - cum
        total = jnp.broadcast_to(cum[:, Q - 1 : Q], (heads, LANES))
        vrow[k] = value
        tots[2 * k] = total
        tots[2 * k + 1] = before
        before = before + total
        tile = jnp.concatenate(
            [cum, jnp.exp2(cum), jnp.exp2(total + value), near, jnp.zeros((Q - 64, LANES), F32)], axis=0
        )
        tile = tile.T
        colf[k] = tile
        hi = tile.astype(BF16)
        cols[k] = jnp.concatenate([hi, (tile - hi.astype(F32)).astype(BF16)], axis=1)
    tots[2 * blocks] = before
    left = iota((pairs, LANES), 1) < 64

    def by_pair(i):
        return jnp.exp2(
            jnp.where(left, tots[i, pl.ds(0, pairs, stride=2), :], tots[i, pl.ds(1, pairs, stride=2), :])
        )

    for k in range(blocks):
        dec_blk[k] = by_pair(2 * k)
        dec_pre[k] = by_pair(2 * k + 1)
    dec_all = by_pair(2 * blocks)
    for p in range(pairs):
        my_dec[p] = dec_all[p : p + 1]

    sel_row = iota((2 * Q, heads * 64), 0)
    sel_head = iota((2 * Q, heads * 64), 1) // 64
    sel_w[...] = ((sel_row == sel_head + 2 * heads) | (sel_row == sel_head + 2 * heads + Q)).astype(F32).astype(BF16)
    sel_e[...] = ((sel_row == sel_head + heads) | (sel_row == sel_head + heads + Q)).astype(F32).astype(BF16)
    row_q, col_q = iota((Q, Q), 0), iota((Q, Q), 1)
    for k in range(blocks):
        reach = jnp.broadcast_to(colf[k, :, 3 * heads + k : 3 * heads + k + 1], (Q, Q))
        pos8[k] = reach[:8]
        shift[k] = jnp.concatenate(
            [
                jnp.where((col_q == row_q - lag) & (reach >= lag), 1.0, 0.0).astype(BF16)
                for lag in range(4)
            ],
            axis=1,
        )

    nxt = lax.rem(me + 1, n_ctx)
    if many:
        pl.semaphore_wait(barrier, n_ctx - 1 + n_head - 1)
        halo_x = pltpu.make_async_remote_copy(
            src_ref=x_hbm.at[pl.ds(rows_all - HALO, HALO), :], dst_ref=hx,
            send_sem=sem_halo_s.at[0], recv_sem=sem_halo_r.at[0],
            device_id={"ctx": nxt}, device_id_type=MESH,
        )
        halo_bc = pltpu.make_async_remote_copy(
            src_ref=bc_hbm.at[pl.ds(rows_all - HALO, HALO), :], dst_ref=hbc,
            send_sem=sem_halo_s.at[1], recv_sem=sem_halo_r.at[1],
            device_id={"ctx": nxt}, device_id_type=MESH,
        )
        halo_x.start()
        halo_bc.start()

        def send_dec(i, _):
            other = lax.rem(me + i, n_ctx)
            pltpu.make_async_remote_copy(
                src_ref=my_dec.at[other // 4], dst_ref=got_dec.at[me],
                send_sem=sem_s.at[0], recv_sem=sem_r.at[0],
                device_id={"ctx": other}, device_id_type=MESH,
            ).start()
            return 0

        lax.fori_loop(1, n_ctx, send_dec, 0)
        got_dec[me] = my_dec[plane]
    else:
        hx[...] = jnp.zeros_like(hx)
        hbc[...] = jnp.zeros_like(hbc)

    load_bc.wait()
    if many:
        halo_bc.wait()
    causal = row_q >= col_q
    bc_taps = [conv_bc[lag] * 0.5 for lag in range(4)]
    for k in range(blocks):
        prev = hbc[...] if k == 0 else bcs[k * Q - HALO : k * Q, :]
        half = conv_block(bcs[k * Q : (k + 1) * Q, :], prev, bc_taps, shift[k], pos8[k])
        bc = twice_silu_half(half)
        b_t = bc[:, :LANES].T.astype(BF16)
        c_mat = bc[:, LANES:].astype(BF16)
        btr[k] = b_t
        cmat[k] = c_mat
        cb[k] = jnp.where(causal, dot(c_mat, b_t), 0.0).astype(BF16)

    for copy in load_x:
        copy.wait()
    if many:
        halo_x.wait()

    def one_quad(i, _):
        q = lax.rem(plane // 2 + i, quads) if many else i
        at = pl.multiple_of(q * QW, QW)
        taps = [conv_x[lag : lag + 1, pl.ds(at, QW)] * 0.5 for lag in range(4)]
        sel = sel_w[:, pl.ds(at, QW)]
        held = jnp.zeros((LANES, QW), F32)
        for k in range(blocks):
            prev = hx[:, pl.ds(at, QW)] if k == 0 else xq[q, k * Q - HALO : k * Q, :]
            half = conv_block(xq[q, k * Q : (k + 1) * Q, :], prev, taps, shift[k], pos8[k])
            act = twice_silu_half(half)
            xc[q, k * Q : (k + 1) * Q, :] = act.astype(BF16)
            weighed = (act * dot(cols[k], sel)).astype(BF16)
            sk[q, k] = held.astype(BF16)
            dec = jnp.concatenate([dec_blk[k, pl.ds(2 * q, 1), :], dec_blk[k, pl.ds(2 * q + 1, 1), :]], axis=1)
            held = held * dec + dot(btr[k], weighed)
        if many:
            for side in range(2):
                p = 2 * q + side
                sbuf[p] = held[:, side * LANES : (side + 1) * LANES].astype(BF16)
                for part in range(4):
                    owner = p * 4 + part

                    @pl.when(owner != me)
                    def _():
                        pltpu.make_async_remote_copy(
                            src_ref=sbuf.at[p, pl.ds(part * part_rows, part_rows), :], dst_ref=got_s.at[me],
                            send_sem=sem_s.at[1], recv_sem=sem_r.at[1],
                            device_id={"ctx": owner}, device_id_type=MESH,
                        ).start()

                    @pl.when(owner == me)
                    def _():
                        got_s[me] = sbuf[p, part * part_rows : (part + 1) * part_rows, :]

        return 0

    lax.fori_loop(0, quads, one_quad, 0)

    for copy in load_z:
        copy.wait()
    left_bf = iota((Q, LANES), 1) < 64

    def one_block(k, _):
        rows = pl.ds(pl.multiple_of(k * Q, Q), Q)
        cb_k = cb[k]
        for q in range(quads):
            out = []
            for side in range(2):
                pair = 2 * q + side
                weights = []
                for h in (2 * pair, 2 * pair + 1):
                    gap = colf[k, :, h : h + 1] + vrow[k, h : h + 1, :]
                    fade = jnp.where(causal, jnp.exp2(gap), 0.0).astype(BF16)
                    weights.append(fade * cb_k)
                x_pair = xc[q, rows, side * LANES : (side + 1) * LANES]
                zero = jnp.zeros_like(x_pair)
                both = jnp.concatenate([jnp.where(left_bf, x_pair, zero), jnp.where(left_bf, zero, x_pair)], axis=0)
                skip = jnp.where(iota((1, LANES), 1) < 64, d_skip[2 * pair], d_skip[2 * pair + 1])
                out.append(dot(jnp.concatenate(weights, axis=1), both) + skip * x_pair.astype(F32))
            ypre[q, rows, :] = jnp.concatenate(out, axis=1)
            z_half = zq[q, rows, :].astype(F32) * 0.5
            gated[q, rows, :] = twice_silu_half(z_half)
        return 0

    lax.fori_loop(0, split, one_block, 0)

    def all_of(sem, like, count):
        view = like.at[pl.ds(0, count)]
        pltpu.make_async_copy(view, view, sem).wait()

    if many:
        all_of(sem_r.at[0], got_dec, n_ctx - 1)
        all_of(sem_r.at[1], got_s, n_ctx - 1)

        def lap(d, acc):
            ret_s[d] = acc.astype(BF16)
            return acc * got_dec[d] + got_s[d].astype(F32)

        lax.fori_loop(0, n_ctx, lap, jnp.zeros((part_rows, LANES), F32), unroll=True)

        def send_back(i, _):
            other = lax.rem(me + i, n_ctx)
            pltpu.make_async_remote_copy(
                src_ref=ret_s.at[other],
                dst_ref=inbound.at[plane, lane_y],
                send_sem=sem_s.at[2], recv_sem=sem_r.at[2],
                device_id={"ctx": other}, device_id_type=MESH,
            ).start()
            return 0

        lax.fori_loop(1, n_ctx, send_back, 0)
        inbound[plane, lane_y] = ret_s[me]

    lax.fori_loop(split, blocks, one_block, 0)

    if many:
        pltpu.make_async_copy(ret_s.at[pl.ds(0, n_ctx - 1)], ret_s.at[pl.ds(0, n_ctx - 1)], sem_r.at[2]).wait()
    else:
        inbound[...] = jnp.zeros_like(inbound)

    score_acc[...] = jnp.zeros_like(score_acc)
    gain_row = gain[...]

    def finish(k, _):
        rows = pl.ds(pl.multiple_of(k * Q, Q), Q)
        squares = jnp.zeros((Q, LANES), F32)
        for q in range(quads):
            dec = jnp.concatenate([dec_pre[k, 2 * q : 2 * q + 1, :], dec_pre[k, 2 * q + 1 : 2 * q + 2, :]], axis=1)
            came = jnp.concatenate(
                [inbound[2 * q].reshape(LANES, LANES), inbound[2 * q + 1].reshape(LANES, LANES)], axis=1
            ).astype(F32)
            start = (sk[q, k].astype(F32) + dec * came).astype(BF16)
            carried = dot(cmat[k], start) * dot(cols[k], sel_e[:, q * QW : (q + 1) * QW])
            value = (ypre[q, rows, :] + carried) * gated[q, rows, :]
            ypre[q, rows, :] = value
            square = value * value
            squares = squares + square[:, :LANES] + square[:, LANES:]
        inv = lax.rsqrt(jnp.sum(squares, axis=1, keepdims=True) * (1.0 / (heads * 64)) + 1e-05)
        for q in range(quads):
            mixed = ypre[q, rows, :] * inv * gain_row[:, q * QW : (q + 1) * QW]
            stage[rows, q * QW : (q + 1) * QW] = mixed.astype(BF16)
        pltpu.make_async_copy(stage.at[rows, :], out_hbm.at[rows, :], sem_out).start()
        spot = me * rows_all + k * Q + iota((CHUNK_ROWS, LANES), 1)
        pick = jnp.where(ends == spot, 1.0, 0.0).astype(BF16)
        score_acc[...] += dot(pick, stage[rows, :])
        return 0

    lax.fori_loop(0, blocks, finish, 0)

    score = jnp.sum(score_acc[...] * readout[...].astype(F32), axis=1, keepdims=True)
    diag = iota((CHUNK_ROWS, LANES), 0) == iota((CHUNK_ROWS, LANES), 1)
    score_row = jnp.sum(jnp.where(diag, score, 0.0), axis=0, keepdims=True)
    if many:
        sc_mine[0] = score_row

        def to_head(i, _):
            other = lax.rem(me_head + i, n_head)
            pltpu.make_async_remote_copy(
                src_ref=sc_mine.at[0], dst_ref=got_h.at[me_head],
                send_sem=sem_s.at[3], recv_sem=sem_r.at[3],
                device_id={"head": other}, device_id_type=MESH,
            ).start()
            return 0

        lax.fori_loop(1, n_head, to_head, 0)
        got_h[me_head] = score_row
        all_of(sem_r.at[3], got_h, n_head - 1)
        score_row = jnp.sum(got_h[...], axis=0)
        sc_ctx[0] = score_row

        def to_ctx(i, _):
            other = lax.rem(me + i, n_ctx)
            pltpu.make_async_remote_copy(
                src_ref=sc_ctx.at[0], dst_ref=got_c.at[me],
                send_sem=sem_s.at[4], recv_sem=sem_r.at[4],
                device_id={"ctx": other}, device_id_type=MESH,
            ).start()
            return 0

        lax.fori_loop(1, n_ctx, to_ctx, 0)
        got_c[me] = score_row
        all_of(sem_r.at[4], got_c, n_ctx - 1)
        score_row = jnp.sum(got_c[...], axis=0)
        all_of(sem_s.at[0], got_dec, n_ctx - 1)
        all_of(sem_s.at[1], got_s, n_ctx - 1)
        all_of(sem_s.at[2], got_s, n_ctx - 1)
        all_of(sem_s.at[3], got_h, n_head - 1)
        all_of(sem_s.at[4], got_c, n_ctx - 1)
    score_ref[...] = score_row
    pltpu.make_async_copy(stage, out_hbm, sem_out).wait()


def local(n_ctx, n_head, x_in, gate_z, bc_in, dt_raw, conv_x, conv_bc, dt_bias, a_log, d_skip, norm_gain, readout, lengths):
    rows, width = x_in.shape
    heads = dt_raw.shape[1]
    blocks, quads, pairs = rows // Q, width // QW, heads // 2
    smem = pl.BlockSpec(memory_space=pltpu.SMEM)
    vmem = pl.BlockSpec(memory_space=pltpu.VMEM)
    hbm = pl.BlockSpec(memory_space=pl.ANY)
    dma = pltpu.SemaphoreType.DMA
    scratch = [
        pltpu.VMEM((quads, rows, QW), BF16),
        pltpu.VMEM((rows, 256), BF16),
        pltpu.VMEM((quads, rows, QW), BF16),
        pltpu.VMEM((HALO, width), BF16),
        pltpu.VMEM((HALO, 256), BF16),
        pltpu.VMEM((blocks, Q, 4 * Q), BF16),
        pltpu.VMEM((blocks, 8, LANES), F32),
        pltpu.VMEM((blocks, Q, 2 * Q), BF16),
        pltpu.VMEM((blocks, Q, Q), F32),
        pltpu.VMEM((blocks, heads, LANES), F32),
        pltpu.VMEM((2 * blocks + 1, heads, LANES), F32),
        pltpu.VMEM((blocks, pairs, LANES), F32),
        pltpu.VMEM((blocks, pairs, LANES), F32),
        pltpu.VMEM((2 * Q, width), BF16),
        pltpu.VMEM((2 * Q, width), BF16),
        pltpu.VMEM((quads, rows, QW), BF16),
        pltpu.VMEM((blocks, Q, LANES), BF16),
        pltpu.VMEM((blocks, LANES, Q), BF16),
        pltpu.VMEM((blocks, Q, Q), BF16),
        pltpu.VMEM((quads, blocks, LANES, QW), BF16),
        pltpu.VMEM((LANES, QW), F32),
        pltpu.VMEM((pairs, LANES, LANES), BF16),
        pltpu.VMEM((quads, rows, QW), F32),
        pltpu.VMEM((quads, rows, QW), F32),
        pltpu.VMEM((rows, width), BF16),
        pltpu.VMEM((CHUNK_ROWS, width), F32),
        pltpu.VMEM((pairs, 1, LANES), F32),
        pltpu.VMEM((n_ctx, 1, LANES), F32),
        pltpu.VMEM((n_ctx, Q // 4, LANES), BF16),
        pltpu.VMEM((n_ctx, Q // 4, LANES), BF16),
        pltpu.VMEM((pairs, 4, Q // 4, LANES), BF16),
        pltpu.VMEM((1, 1, LANES), F32),
        pltpu.VMEM((1, 1, LANES), F32),
        pltpu.VMEM((n_head, 1, LANES), F32),
        pltpu.VMEM((n_ctx, 1, LANES), F32),
        dma((quads,)), dma, dma((quads,)), dma, dma((2,)), dma((2,)), dma((5,)), dma((5,)),
    ]
    params = dict(vmem_limit_bytes=60 * 1024 * 1024)
    if n_ctx > 1:
        params.update(collective_id=0, has_side_effects=True)
    split = min(4, blocks)
    mixed, score = pl.pallas_call(
        functools.partial(kernel, (n_ctx, n_head, rows, heads, split)),
        out_shape=(jax.ShapeDtypeStruct((rows, width), BF16), jax.ShapeDtypeStruct((1, LANES), F32)),
        in_specs=[smem] * 4 + [vmem] * 5 + [hbm] * 3,
        out_specs=(hbm, vmem),
        scratch_shapes=scratch,
        compiler_params=pltpu.CompilerParams(**params),
    )(
        lengths, dt_bias, a_log, d_skip,
        dt_raw.T, conv_x, conv_bc, norm_gain.reshape(1, width), readout.reshape(1, width),
        x_in, gate_z, bc_in.reshape(rows, bc_in.shape[2]),
    )
    return mixed, score.reshape(LANES)[: lengths.shape[0]]


def solution(mesh):
    in_specs = (
        P("ctx", "head"),
        P("ctx", "head"),
        P("ctx", "head", None),
        P("ctx", "head"),
        P(None, "head"),
        P(None, "head", None),
        P("head"),
        P("head"),
        P("head"),
        P("head"),
        P("head"),
        P(),
    )
    out_specs = (P("ctx", "head"), P())
    step = functools.partial(local, mesh.shape["ctx"], mesh.shape["head"])
    return jax.shard_map(step, mesh=mesh, in_specs=in_specs, out_specs=out_specs, check_vma=False)
```

time: 447 us -> 67.9 us (0.15)
  blocking collectives: 112 us -> 0 us
  waiting for transfers between devices: 98 us -> 0 us
  other arithmetic: 82.4 us -> 0 us
  matrix products: 68.8 us -> 0 us
  Pallas kernels: 0 us -> 60.8 us
  local copies, waits for them, and re-layouts: 56.3 us -> 6.26 us
  between operations: 14.2 us -> 0.64 us
  starting transfers between devices: 7.25 us -> 0 us
  loops' own time: 5.55 us -> 0 us
    all_gather x1 -> x0, waiting for transfers between devices: 98 us -> none  [prefix(): everything = jax.tree.map(lambda part: lax.all_gather(part, axis), x)]
    psum x1 -> x0, blocking collectives: 74.9 us -> none  [local(): cand_scores = lax.psum(partial_sum, ('ctx', 'head'))]
    dot_general x27 -> x0, matrix products: 68.8 us -> none  [the longest x6 28.7 us: block_ssd(): jnp.einsum('hts,shp->thp', weights_mat, x_conv, precision=HIGHEST_PREC)]
    pallas_call x0 -> x1, Pallas kernels: none -> 60.8 us  [local(): pl.pallas_call(functools.partial(kernel, (n_ctx, n_head, rows, heads, spl...]
    select_n x32 -> x0, other arithmetic: 37.7 us -> none  [lap(): return jax.tree.map(lambda a, b: jnp.where(reached, a, b), new, before)]
    all_gather x1 -> x0, blocking collectives: 36.6 us -> none  [prefix(): everything = jax.tree.map(lambda part: lax.all_gather(part, axis), x)]
    mul x17 -> x0, other arithmetic: 22.3 us -> none  [the longest x2 16.4 us: causal_conv(): return jax.nn.silu(conv_sum)]
    dynamic_slice x30 -> x0, local copies, waits for them, and re-layouts: 15.5 us -> none  [local(): (state_dev, _), y_blocks = lax.scan(block_step, carry_start, blocks_in)]
  transfers between devices with their start and end apart: 3 -> 0, of which waited for: 1 -> 0; matrix products, arithmetic and copies ran while one was open for 5% -> 0% of each run, Pallas kernels for 0% -> 0%
where the time goes in v1:
time: 67.9 us; the launch traced here: 67.7 us
  Pallas kernels  60.8 us (90%)
  local copies, waits for them, and re-layouts  6.26 us (9%)
    pallas_call x1, Pallas kernels, local(): pl.pallas_call(functools.partial(kernel, (n_ctx, n_head, rows, heads, spl...  60.8 us
    unnamed x1, local copies, waits for them, and re-layouts  3.86 us

profile of v1, /device:TPU:1, one launch (start us, length us, event | category | flops | bytes accessed | tf_op | source)
XLA Modules:
  0.0 67.7 jit_solution(11569928002601678377)
XLA Ops:
  0.6 1.3 %reshape.16.readout = bf16[1,1024]{1,0:T(2,128)(2,1)} reshape(bf16[1024]{0:T(1024)(128)(2,1)} %param.22) | data formatting | bytes 4096 | tf_op jit(solution)/shard_map/reshape | solution.py:470
  1.9 60.8 %shard_map.131 = (bf16[1536,1024]{1,0:T(8,128)(2,1)}, f32[1,128]{1,0:T(1,128)}) custom-call(s32[16]{0:T(128)} %lengths.1, f32[16]{0:T(128)} %bias.1, f32[16]{0:T(128)} %a_log.1, f32[16]{0:T(128)} %d_skip.1, f32[16,1536]{1,0:T(8,128)} %bitcast.6, f32[4,1024]{1,0:T(4,128)} %conv_x.1, f32[4,1,256]{2,1,0:T(1,128)} %conv_bc.1, f32[1,1024]{1,0:T(1,128)} %bitcast.7, ...), custom_call_target="tpu_custom_call" | custom-call | tf_op jit(solution)/shard_map/pallas_call | solution.py:461
  62.7 1.1 %slice_bitcast_fusion = f32[16]{0:T(128)} fusion(f32[1,128]{1,0:T(1,128)} %get-tuple-element.5), kind=kLoop, calls=%fused_computation | loop fusion | bytes 128 | tf_op jit(solution)/shard_map/slice | solution.py:473
  63.9 3.9 %copy.15 = bf16[1536,1024]{1,0:T(8,128)(2,1)} copy(bf16[1536,1024]{1,0:T(8,128)(2,1)} %get-tuple-element.8) | data formatting | bytes 6291456

commit v2 on v1

v2 whole, which is shorter than its diff:
```python
import functools

import jax
import jax.numpy as jnp
from jax import lax
from jax.experimental import pallas as pl
from jax.experimental.pallas import tpu as pltpu
from jax.sharding import PartitionSpec as P

F32, BF16, I32 = jnp.float32, jnp.bfloat16, jnp.int32
MESH = pl.DeviceIdType.MESH
LOG2E = 1.4426950408889634
Q = 128
QW = 256
HALO = 16
RESET = 200.0
LANES = 128
TABLE = 16
PART = 32
MSG = PART + 16


def iota(shape, dim):
    return lax.broadcasted_iota(I32, shape, dim)


def dot(a, b):
    return jnp.dot(a, b, preferred_element_type=F32)


def dot_t(a, b):
    return lax.dot_general(a, b, (((0,), (0,)), ((), ())), preferred_element_type=F32)


def two(x):
    hi = x.astype(BF16)
    return hi, (x - hi.astype(F32)).astype(BF16)


def three(x):
    hi = x.astype(BF16)
    return (hi,) + two(x - hi.astype(F32))


def softplus(v):
    u = jnp.exp(-jnp.abs(v))
    small = u * (1.0 + u * (-0.5 + u * (1.0 / 3.0 - 0.25 * u)))
    return jnp.maximum(v, 0.0) + jnp.where(u < 0.01, small, jnp.log(1.0 + u))


def twice_silu_half(h):
    return h + h * jnp.tanh(h)


def half_conv(rows, before, taps, keep):
    x = jnp.concatenate([before.astype(F32)[HALO - 8 :], rows.astype(F32)], axis=0)
    keep = jnp.concatenate([keep] * (x.shape[1] // LANES), axis=1)
    acc = x * taps[3]
    for lag in (2, 1, 0):
        acc = pltpu.roll(acc, 1, 0) * keep + x * taps[lag]
    return acc[8:]


def kernel(
    dims,
    lengths_hbm, bias_hbm, a_log_hbm, d_skip_hbm,
    dt_hbm, conv_x_hbm, conv_bc_hbm, gain_hbm, readout_hbm, x_hbm, z_hbm, bc_hbm,
    out_hbm, score_ref,
    lengths, bias, a_log, d_skip, dt_ref, conv_x, conv_bc, gain, readout,
    xq, bcs, zq, hx, hbc, keep, colf, vrow, whl, ehl, tots, dec_blk, dec_pre, sel,
    xc, cmat, cwide, btr, cb, sk, fresh, dec_one, sbuf, part_a, part_b, stage, sin, end_a, end_b, end_c,
    got_s, ret_s, inbound, sc_mine, sc_ctx, got_h, got_c,
    sem_small, sem_x, sem_bc, sem_z, sem_out, sem_halo_s, sem_halo_r, sem_s, sem_r,
):
    n_ctx, n_head, rows_all, heads, split = dims
    blocks = rows_all // Q
    quads = heads * 64 // QW
    pairs = heads // 2
    many = n_ctx > 1
    me = lax.axis_index("ctx")
    me_head = lax.axis_index("head")
    plane, lane_y = me // 4, me % 4

    load_small = [
        pltpu.make_async_copy(source, target, sem_small.at[i])
        for i, (source, target) in enumerate(
            [
                (lengths_hbm, lengths), (bias_hbm, bias), (a_log_hbm, a_log), (d_skip_hbm, d_skip),
                (dt_hbm, dt_ref), (conv_x_hbm, conv_x), (conv_bc_hbm, conv_bc), (gain_hbm, gain), (readout_hbm, readout),
            ]
        )
    ]
    for copy in load_small:
        copy.start()
    load_bc = pltpu.make_async_copy(bc_hbm, bcs, sem_bc)
    load_bc.start()
    load_x = [
        pltpu.make_async_copy(x_hbm.at[:, pl.ds(q * QW, QW)], xq.at[q], sem_x.at[q])
        for q in range(quads)
    ]
    load_z = [
        pltpu.make_async_copy(z_hbm.at[:, pl.ds(q * QW, QW)], zq.at[q], sem_z.at[q])
        for q in range(quads)
    ]
    for copy in load_x + load_z:
        copy.start()

    if many:
        barrier = pltpu.get_barrier_semaphore()

        def greet_ctx(i, _):
            pl.semaphore_signal(barrier, inc=1, device_id={"ctx": lax.rem(me + i, n_ctx)}, device_id_type=MESH)
            return 0

        lax.fori_loop(1, n_ctx, greet_ctx, 0)

        def greet_head(i, _):
            pl.semaphore_signal(barrier, inc=1, device_id={"head": lax.rem(me_head + i, n_head)}, device_id_type=MESH)
            return 0

        lax.fori_loop(1, n_head, greet_head, 0)

    for copy in load_small:
        copy.wait()

    offset = jnp.int32(0)
    here = me * rows_all + (iota((TABLE, LANES), 0) - 1) * Q + iota((TABLE, LANES), 1)
    first = jnp.zeros((TABLE, LANES), F32)
    ends = []
    for c in range(lengths.shape[0]):
        first = jnp.where(here == offset, 1.0, first)
        offset = offset + lengths[c]
        ends.append(offset - 1)

    head_row = iota((heads, LANES), 0)
    bias_col = jnp.zeros((heads, LANES), F32)
    rate_col = jnp.zeros((heads, LANES), F32)
    for h in range(heads):
        bias_col = jnp.where(head_row == h, bias[h], bias_col)
        rate_col = jnp.where(head_row == h, a_log[h], rate_col)
    rate_col = jnp.exp(rate_col) * (-LOG2E)
    steps, logs = [], []
    for k in range(blocks):
        dt_vals = softplus(dt_ref[:, k * Q : (k + 1) * Q] + bias_col)
        steps.append(jnp.log(dt_vals) * LOG2E)
        logs.append(dt_vals * rate_col - RESET * first[k + 1 : k + 2])
    upper = (iota((Q, Q), 0) <= iota((Q, Q), 1)).astype(F32).astype(BF16)
    cum_all = dot(
        jnp.concatenate(three(jnp.concatenate(logs, axis=0)), axis=1),
        jnp.concatenate([upper] * 3, axis=0),
    )
    before = jnp.zeros((heads, LANES), F32)
    for k in range(blocks):
        cum = cum_all[k * heads : (k + 1) * heads]
        value = steps[k] - cum
        total = jnp.broadcast_to(cum[:, Q - 1 : Q], (heads, LANES))
        vrow[k] = value
        colf[k, :heads] = cum
        whl[k] = jnp.concatenate(two(jnp.exp2(total + value)), axis=0)
        tots[2 * k] = total
        tots[2 * k + 1] = before
        before = before + total
    tots[2 * blocks] = before
    left = iota((pairs, LANES), 1) < 64

    def by_pair(i):
        return jnp.where(left, tots[i, pl.ds(0, pairs, stride=2), :], tots[i, pl.ds(1, pairs, stride=2), :])

    one_on = by_pair(3)
    for k in range(blocks):
        dec_blk[k] = jnp.exp2(by_pair(2 * k))
    dec_one[blocks] = jnp.exp2(by_pair(2 * blocks) - one_on)

    sel_row, sel_head = iota((2 * heads, heads * 64), 0), iota((2 * heads, heads * 64), 1) // 64
    sel[...] = jnp.where((sel_row == sel_head) | (sel_row == sel_head + heads), 1.0, 0.0).astype(BF16)
    keep_col = jnp.concatenate([1.0 - first, jnp.zeros((LANES - TABLE, LANES), F32)], axis=0).T
    for k in range(blocks + 1):
        keep[k * Q : (k + 1) * Q, :] = jnp.broadcast_to(keep_col[:, k : k + 1], (Q, LANES))

    load_bc.wait()
    bc_taps = [conv_bc[lag] * 0.5 for lag in range(4)]

    def conv_bc_block(k, at):
        prev = hbc[:, at : at + LANES] if k == 0 else bcs[k * Q - HALO : k * Q, at : at + LANES]
        half = half_conv(
            bcs[k * Q : (k + 1) * Q, at : at + LANES], prev,
            [tap[:, at : at + LANES] for tap in bc_taps], keep[(k + 1) * Q - 8 : (k + 2) * Q, :],
        )
        return twice_silu_half(half)

    if many:
        dec_all = jnp.exp2(by_pair(2 * blocks))
        part_row = iota((16, LANES), 0)
        for p in range(pairs):
            hi, mid, low = (v.astype(F32) for v in three(dec_all[p : p + 1]))
            tile = jnp.where(part_row == 0, hi, jnp.where(part_row == 1, mid, jnp.where(part_row == 2, low, 0.0)))
            for part in range(4):
                sbuf[p, part, PART:, :] = tile.astype(BF16)

    for k in range(1, blocks):
        btr[k] = conv_bc_block(k, 0).T.astype(BF16)

    nxt = lax.rem(me + 1, n_ctx)
    if many:
        pl.semaphore_wait(barrier, n_ctx - 1 + n_head - 1)
        halo_x = pltpu.make_async_remote_copy(
            src_ref=x_hbm.at[pl.ds(rows_all - HALO, HALO), :], dst_ref=hx,
            send_sem=sem_halo_s.at[0], recv_sem=sem_halo_r.at[0],
            device_id={"ctx": nxt}, device_id_type=MESH,
        )
        halo_bc = pltpu.make_async_remote_copy(
            src_ref=bc_hbm.at[pl.ds(rows_all - HALO, HALO), :], dst_ref=hbc,
            send_sem=sem_halo_s.at[1], recv_sem=sem_halo_r.at[1],
            device_id={"ctx": nxt}, device_id_type=MESH,
        )
        halo_x.start()
        halo_bc.start()
    else:
        hx[...] = jnp.zeros_like(hx)
        hbc[...] = jnp.zeros_like(hbc)

    for copy in load_x:
        copy.wait()

    def one_quad(i, _):
        q = lax.rem(plane // 2 + i, quads) if many else i
        at = pl.multiple_of(q * QW, QW)
        taps = [conv_x[lag : lag + 1, pl.ds(at, QW)] * 0.5 for lag in range(4)]
        pick = sel[:, pl.ds(at, QW)]

        def weighed_block(k):
            prev = hx[:, pl.ds(at, QW)] if k == 0 else xq[q, k * Q - HALO : k * Q, :]
            half = half_conv(xq[q, k * Q : (k + 1) * Q, :], prev, taps, keep[(k + 1) * Q - 8 : (k + 2) * Q, :])
            act = twice_silu_half(half)
            xc[q, k * Q : (k + 1) * Q, :] = act.astype(BF16)
            return (act * dot_t(whl[k], pick)).astype(BF16)

        def by_quad(ref, k):
            return jnp.concatenate([ref[k, pl.ds(2 * q, 1), :], ref[k, pl.ds(2 * q + 1, 1), :]], axis=1)

        held = dot(btr[1], weighed_block(1))
        for k in range(2, blocks):
            weighed = weighed_block(k)
            sk[q, k] = held.astype(BF16)
            held = held * by_quad(dec_blk, k) + dot(btr[k], weighed)

        @pl.when(i == 0)
        def _():
            if many:
                halo_x.wait()
                halo_bc.wait()
            btr[0] = conv_bc_block(0, 0).T.astype(BF16)

        block0 = dot(btr[0], weighed_block(0))
        fresh[q] = block0
        held = held + block0 * by_quad(dec_one, blocks)
        if many:
            for side in range(2):
                p = 2 * q + side
                for part in range(4):
                    owner = p * 4 + part
                    sbuf[p, part, :PART, :] = held[
                        part * PART : (part + 1) * PART, side * LANES : (side + 1) * LANES
                    ].astype(BF16)

                    @pl.when(owner != me)
                    def _():
                        pltpu.make_async_remote_copy(
                            src_ref=sbuf.at[p, part], dst_ref=got_s.at[me],
                            send_sem=sem_s.at[0], recv_sem=sem_r.at[0],
                            device_id={"ctx": owner}, device_id_type=MESH,
                        ).start()

                    @pl.when(owner == me)
                    def _():
                        got_s[me] = sbuf[p, part]

        return 0

    lax.fori_loop(0, quads, one_quad, 0)

    causal = iota((Q, Q), 0) >= iota((Q, Q), 1)
    for k in range(blocks):
        c_wide = conv_bc_block(k, LANES)
        c_mat = c_wide.astype(BF16)
        cwide[k * Q : (k + 1) * Q, :] = c_wide
        cmat[k * Q : (k + 1) * Q, :] = c_mat
        cb[k] = jnp.where(causal, dot(c_mat, btr[k]), 0.0).astype(BF16)
        cum = colf[k, :heads]
        ehl[k] = jnp.concatenate(two(jnp.exp2(cum)), axis=0)
        colf[k] = jnp.concatenate([cum, jnp.zeros((Q - heads, LANES), F32)], axis=0).T
        log_pre = by_pair(2 * k + 1)
        dec_pre[k] = jnp.exp2(log_pre)
        dec_one[k] = jnp.exp2(log_pre - one_on) if k else jnp.zeros_like(log_pre)
    for q in range(quads):
        sk[q, 0] = jnp.zeros((LANES, QW), BF16)
        sk[q, 1] = jnp.zeros((LANES, QW), BF16)

    for copy in load_z:
        copy.wait()
    left_bf = iota((Q, LANES), 1) < 64

    def one_block(k, _):
        rows = pl.ds(pl.multiple_of(k * Q, Q), Q)
        cb_k = cb[k]
        c_k = cmat[rows, :]
        for q in range(quads):
            out = []
            for side in range(2):
                pair = 2 * q + side
                weights = []
                for h in (2 * pair, 2 * pair + 1):
                    gap = colf[k, :, h : h + 1] + vrow[k, h : h + 1, :]
                    fade = jnp.where(causal, jnp.exp2(gap), 0.0).astype(BF16)
                    weights.append(fade * cb_k)
                x_pair = xc[q, rows, side * LANES : (side + 1) * LANES]
                zero = jnp.zeros_like(x_pair)
                both = jnp.concatenate([jnp.where(left_bf, x_pair, zero), jnp.where(left_bf, zero, x_pair)], axis=0)
                skip = jnp.where(iota((1, LANES), 1) < 64, d_skip[2 * pair], d_skip[2 * pair + 1])
                out.append(dot(jnp.concatenate(weights, axis=1), both) + skip * x_pair.astype(F32))
            fade_in = dot_t(ehl[k], sel[:, q * QW : (q + 1) * QW])
            since = jnp.concatenate([dec_one[k, 2 * q : 2 * q + 1, :], dec_one[k, 2 * q + 1 : 2 * q + 2, :]], axis=1)
            start = (sk[q, k].astype(F32) + since * fresh[q]).astype(BF16)
            inside = jnp.concatenate(out, axis=1) + fade_in * dot(c_k, start)
            gate = twice_silu_half(zq[q, rows, :].astype(F32) * 0.5)
            dec = jnp.concatenate([dec_pre[k, 2 * q : 2 * q + 1, :], dec_pre[k, 2 * q + 1 : 2 * q + 2, :]], axis=1)
            part_a[q, rows, :] = inside * gate
            part_b[q, rows, :] = fade_in * dec * gate
        return 0

    lax.fori_loop(0, split, one_block, 0)

    def all_of(sem, like, count):
        view = like.at[pl.ds(0, count)]
        pltpu.make_async_copy(view, view, sem).wait()

    if many:
        all_of(sem_r.at[0], got_s, n_ctx - 1)

        def lap(d, acc):
            ret_s[d] = acc.astype(BF16)
            dec = jnp.sum(got_s[d, PART:, :].astype(F32), axis=0, keepdims=True)
            return acc * dec + got_s[d, :PART, :].astype(F32)

        lax.fori_loop(0, n_ctx, lap, jnp.zeros((PART, LANES), F32), unroll=True)

        def send_back(i, _):
            other = lax.rem(me + i, n_ctx)
            pltpu.make_async_remote_copy(
                src_ref=ret_s.at[other], dst_ref=inbound.at[plane, lane_y],
                send_sem=sem_s.at[1], recv_sem=sem_r.at[1],
                device_id={"ctx": other}, device_id_type=MESH,
            ).start()
            return 0

        lax.fori_loop(1, n_ctx, send_back, 0)
        inbound[plane, lane_y] = ret_s[me]

    lax.fori_loop(split, blocks, one_block, 0)

    for c, end in enumerate(ends):
        spot = end - me * rows_all
        mine = jnp.where((spot >= 0) & (spot < rows_all), 1.0, 0.0)
        spot = jnp.minimum(jnp.maximum(spot, 0), rows_all - 1)
        end_c[c : c + 1, :] = cwide[pl.ds(spot, 1), :]
        for q in range(quads):
            end_a[c : c + 1, q * QW : (q + 1) * QW] = part_a[q, pl.ds(spot, 1), :] * mine
            end_b[c : c + 1, q * QW : (q + 1) * QW] = part_b[q, pl.ds(spot, 1), :] * mine

    if many:
        all_of(sem_r.at[1], ret_s, n_ctx - 1)
    else:
        inbound[...] = jnp.zeros_like(inbound)
    for p in range(pairs):
        sin[:, p * LANES : (p + 1) * LANES] = inbound[p].reshape(LANES, LANES)

    last = end_a[...] + end_b[...] * dot(end_c[...].astype(BF16), sin[...])
    width = heads * 64
    inv = lax.rsqrt(jnp.sum(last * last, axis=1, keepdims=True) * (1.0 / width) + 1e-05)
    rounded = (last * inv * gain[...].reshape(1, width)).astype(BF16).astype(F32)
    score = jnp.sum(rounded * readout[...].astype(F32).reshape(1, width), axis=1, keepdims=True)
    diag = iota((TABLE, LANES), 0) == iota((TABLE, LANES), 1)
    score_row = jnp.sum(jnp.where(diag, score, 0.0), axis=0, keepdims=True)
    if many:
        sc_mine[0] = score_row

        def to_head(i, _):
            pltpu.make_async_remote_copy(
                src_ref=sc_mine.at[0], dst_ref=got_h.at[me_head],
                send_sem=sem_s.at[2], recv_sem=sem_r.at[2],
                device_id={"head": lax.rem(me_head + i, n_head)}, device_id_type=MESH,
            ).start()
            return 0

        lax.fori_loop(1, n_head, to_head, 0)
        got_h[me_head] = score_row

    def finish(k, _):
        rows = pl.ds(pl.multiple_of(k * Q, Q), Q)
        c_k = cmat[rows, :]
        squares = jnp.zeros((Q, LANES), F32)
        for q in range(quads):
            value = part_a[q, rows, :] + part_b[q, rows, :] * dot(c_k, sin[:, q * QW : (q + 1) * QW])
            part_a[q, rows, :] = value
            square = value * value
            squares = squares + square[:, :LANES] + square[:, LANES:]
        inv = lax.rsqrt(jnp.sum(squares, axis=1, keepdims=True) * (1.0 / width) + 1e-05)
        gain_row = gain[...].reshape(1, width)
        for q in range(quads):
            mixed = part_a[q, rows, :] * inv * gain_row[:, q * QW : (q + 1) * QW]
            stage[rows, q * QW : (q + 1) * QW] = mixed.astype(BF16)
        pltpu.make_async_copy(stage.at[rows, :], out_hbm.at[rows, :], sem_out).start()
        return 0

    lax.fori_loop(0, blocks // 2, finish, 0)
    if many:
        all_of(sem_r.at[2], got_h, n_head - 1)
        score_row = jnp.sum(got_h[...], axis=0)
        sc_ctx[0] = score_row

        def to_ctx(i, _):
            pltpu.make_async_remote_copy(
                src_ref=sc_ctx.at[0], dst_ref=got_c.at[me],
                send_sem=sem_s.at[3], recv_sem=sem_r.at[3],
                device_id={"ctx": lax.rem(me + i, n_ctx)}, device_id_type=MESH,
            ).start()
            return 0

        lax.fori_loop(1, n_ctx, to_ctx, 0)
        got_c[me] = score_row
    lax.fori_loop(blocks // 2, blocks, finish, 0)
    if many:
        all_of(sem_s.at[0], got_s, n_ctx - 1)
        all_of(sem_s.at[1], ret_s, n_ctx - 1)
        all_of(sem_s.at[2], got_h, n_head - 1)
        all_of(sem_s.at[3], got_c, n_ctx - 1)
        all_of(sem_r.at[3], got_c, n_ctx - 1)
        score_row = jnp.sum(got_c[...], axis=0)
    score_ref[...] = score_row[0, : score_ref.shape[0]]
    pltpu.make_async_copy(stage, out_hbm, sem_out).wait()


def local(n_ctx, n_head, x_in, gate_z, bc_in, dt_raw, conv_x, conv_bc, dt_bias, a_log, d_skip, norm_gain, readout, lengths):
    rows, width = x_in.shape
    heads = dt_raw.shape[1]
    blocks, quads, pairs = rows // Q, width // QW, heads // 2
    vmem = pl.BlockSpec(memory_space=pltpu.VMEM)
    anywhere = pl.BlockSpec(memory_space=pl.ANY)
    hbm = pl.BlockSpec(memory_space=pltpu.HBM)
    dma = pltpu.SemaphoreType.DMA
    scratch = [
        pltpu.SMEM(lengths.shape, I32),
        pltpu.SMEM(dt_bias.shape, F32),
        pltpu.SMEM(a_log.shape, F32),
        pltpu.SMEM(d_skip.shape, F32),
        pltpu.VMEM((heads, rows), F32),
        pltpu.VMEM(conv_x.shape, F32),
        pltpu.VMEM(conv_bc.shape, F32),
        pltpu.VMEM(norm_gain.shape, F32),
        pltpu.VMEM(readout.shape, BF16),
        pltpu.VMEM((quads, rows, QW), BF16),
        pltpu.VMEM((rows, 256), BF16),
        pltpu.VMEM((quads, rows, QW), BF16),
        pltpu.VMEM((HALO, width), BF16),
        pltpu.VMEM((HALO, 256), BF16),
        pltpu.VMEM((rows + Q, LANES), F32),
        pltpu.VMEM((blocks, Q, Q), F32),
        pltpu.VMEM((blocks, heads, LANES), F32),
        pltpu.VMEM((blocks, 2 * heads, LANES), BF16),
        pltpu.VMEM((blocks, 2 * heads, LANES), BF16),
        pltpu.VMEM((2 * blocks + 1, heads, LANES), F32),
        pltpu.VMEM((blocks, pairs, LANES), F32),
        pltpu.VMEM((blocks, pairs, LANES), F32),
        pltpu.VMEM((2 * heads, width), BF16),
        pltpu.VMEM((quads, rows, QW), BF16),
        pltpu.VMEM((rows, LANES), BF16),
        pltpu.VMEM((rows, LANES), F32),
        pltpu.VMEM((blocks, LANES, Q), BF16),
        pltpu.VMEM((blocks, Q, Q), BF16),
        pltpu.VMEM((quads, blocks, LANES, QW), BF16),
        pltpu.VMEM((quads, LANES, QW), F32),
        pltpu.VMEM((blocks + 1, pairs, LANES), F32),
        pltpu.VMEM((pairs, 4, MSG, LANES), BF16),
        pltpu.VMEM((quads, rows, QW), F32),
        pltpu.VMEM((quads, rows, QW), F32),
        pltpu.VMEM((rows, width), BF16),
        pltpu.VMEM((LANES, width), BF16),
        pltpu.VMEM((TABLE, width), F32),
        pltpu.VMEM((TABLE, width), F32),
        pltpu.VMEM((TABLE, LANES), F32),
        pltpu.VMEM((n_ctx, MSG, LANES), BF16),
        pltpu.VMEM((n_ctx, PART, LANES), BF16),
        pltpu.VMEM((pairs, 4, PART, LANES), BF16),
        pltpu.VMEM((1, 1, LANES), F32),
        pltpu.VMEM((1, 1, LANES), F32),
        pltpu.VMEM((n_head, 1, LANES), F32),
        pltpu.VMEM((n_ctx, 1, LANES), F32),
        dma((9,)), dma((quads,)), dma, dma((quads,)), dma, dma((2,)), dma((2,)), dma((4,)), dma((4,)),
    ]
    params = dict(vmem_limit_bytes=50 * 1024 * 1024)
    if n_ctx > 1:
        params.update(collective_id=0, has_side_effects=True)
    split = min(3, blocks)
    return pl.pallas_call(
        functools.partial(kernel, (n_ctx, n_head, rows, heads, split)),
        out_shape=(jax.ShapeDtypeStruct((rows, width), BF16), jax.ShapeDtypeStruct(lengths.shape, F32)),
        in_specs=[hbm] * 12,
        out_specs=(anywhere, vmem),
        scratch_shapes=scratch,
        compiler_params=pltpu.CompilerParams(**params),
    )(
        *(
            pltpu.with_memory_space_constraint(array, pltpu.HBM)
            for array in (
                lengths, dt_bias, a_log, d_skip,
                dt_raw.T, conv_x, conv_bc, norm_gain, readout,
                x_in, gate_z, bc_in.reshape(rows, bc_in.shape[2]),
            )
        )
    )


def solution(mesh):
    in_specs = (
        P("ctx", "head"),
        P("ctx", "head"),
        P("ctx", "head", None),
        P("ctx", "head"),
        P(None, "head"),
        P(None, "head", None),
        P("head"),
        P("head"),
        P("head"),
        P("head"),
        P("head"),
        P(),
    )
    out_specs = (P("ctx", "head"), P())
    step = functools.partial(local, mesh.shape["ctx"], mesh.shape["head"])
    return jax.shard_map(step, mesh=mesh, in_specs=in_specs, out_specs=out_specs, check_vma=False)
```

time: 67.9 us -> 51.4 us (0.76)
  Pallas kernels: 60.8 us -> 48.5 us
  local copies, waits for them, and re-layouts: 6.26 us -> 2.18 us
    pallas_call x1, Pallas kernels: 60.8 us -> 48.5 us  [local(): pl.pallas_call(functools.partial(kernel, (n_ctx, n_head, rows, heads, spl...]
    unnamed x1 -> x2, local copies, waits for them, and re-layouts: 3.86 us -> 2.18 us
    reshape x1 -> x0, local copies, waits for them, and re-layouts: 1.28 us -> none  [local(): readout.reshape(1, width)]
    slice x1 -> x0, local copies, waits for them, and re-layouts: 1.12 us -> none  [local(): return (mixed, score.reshape(LANES)[:lengths.shape[0]])]
where the time goes in v2:
time: 51.4 us; the launch traced here: 51.3 us
  Pallas kernels  48.5 us (94%)
  local copies, waits for them, and re-layouts  2.18 us (4%)
  between operations  0.64 us (1%)
    pallas_call x1, Pallas kernels, local(): pl.pallas_call(functools.partial(kernel, (n_ctx, n_head, rows, heads, spl...  48.5 us
    unnamed x2, local copies, waits for them, and re-layouts  2.18 us

profile of v2, /device:TPU:1, one launch (start us, length us, event | category | flops | bytes accessed | tf_op | source)
XLA Modules:
  0.0 51.3 jit_solution(11702518116143422621)
XLA Ops:
  0.6 48.5 %shard_map.131 = (bf16[1536,1024]{1,0:T(8,128)(2,1)S(1)}, f32[16]{0:T(128)S(1)}) custom-call(s32[16]{0:T(128)} %lengths_hbm.1, f32[16]{0:T(128)} %bias_hbm.1, f32[16]{0:T(128)} %a_log_hbm.1, f32[16]{0:T(128)} %d_skip_hbm.1, f32[16,1536]{1,0:T(8,128)} %bitcast.3, f32[4,1024]{1,0:T(4,128)} %conv_x_hbm.1, f32[4,1,256]{2,1,0:T(1,128)} %conv_bc_hbm.1, ...), custom_call_target="tpu_custom_call" | custom-call | tf_op jit(solution)/shard_map/pallas_call | solution.py:504
  49.2 1.7 %copy.16 = bf16[1536,1024]{1,0:T(8,128)(2,1)} copy(bf16[1536,1024]{1,0:T(8,128)(2,1)S(1)} %get-tuple-element.4) | data formatting | bytes 6291456
  50.8 0.5 copy.17

commit v3 on v2

--- a/solution.py
+++ b/solution.py
@@ -16,8 +16,8 @@
 RESET = 200.0
 LANES = 128
 TABLE = 16
-PART = 32
-MSG = PART + 16
+PART = 16
+TILES = LANES // PART
 
 
 def iota(shape, dim):
@@ -52,13 +52,20 @@
     return h + h * jnp.tanh(h)
 
 
-def half_conv(rows, before, taps, keep):
+def half_conv(rows, before, taps, keep, buf, slot):
+    outs = []
+    tiles = rows.shape[1] // LANES
     x = jnp.concatenate([before.astype(F32)[HALO - 8 :], rows.astype(F32)], axis=0)
-    keep = jnp.concatenate([keep] * (x.shape[1] // LANES), axis=1)
-    acc = x * taps[3]
-    for lag in (2, 1, 0):
-        acc = pltpu.roll(acc, 1, 0) * keep + x * taps[lag]
-    return acc[8:]
+    for t in range(tiles):
+        buf[2 * slot + t] = x[:, t * LANES : (t + 1) * LANES]
+    for t in range(tiles):
+        tap = [w[:, t * LANES : (t + 1) * LANES] for w in taps]
+        late = [buf[2 * slot + t, 8 - lag : 8 - lag + Q, :] for lag in (1, 2, 3)]
+        acc = late[2] * tap[3] * keep[2]
+        acc = (acc + late[1] * tap[2]) * keep[1]
+        acc = (acc + late[0] * tap[1]) * keep[0]
+        outs.append(acc + x[8:, t * LANES : (t + 1) * LANES] * tap[0])
+    return outs[0] if tiles == 1 else jnp.concatenate(outs, axis=1)
 
 
 def kernel(
@@ -67,10 +74,10 @@
     dt_hbm, conv_x_hbm, conv_bc_hbm, gain_hbm, readout_hbm, x_hbm, z_hbm, bc_hbm,
     out_hbm, score_ref,
     lengths, bias, a_log, d_skip, dt_ref, conv_x, conv_bc, gain, readout,
-    xq, bcs, zq, hx, hbc, keep, colf, vrow, whl, ehl, tots, dec_blk, dec_pre, sel,
-    xc, cmat, cwide, btr, cb, sk, fresh, dec_one, sbuf, part_a, part_b, stage, sin, end_a, end_b, end_c,
-    got_s, ret_s, inbound, sc_mine, sc_ctx, got_h, got_c,
-    sem_small, sem_x, sem_bc, sem_z, sem_out, sem_halo_s, sem_halo_r, sem_s, sem_r,
+    xq, bcs, zq, hx, hbc, keep, keep2, keep3, buf, colf, vrow, whl, ehl, tots, dec_blk, dec_pre, sel,
+    xc, cmat, cwide, btr, cb, sk, fresh, held_all, dec_one, sbuf, part_a, part_b, stage, sin, end_a, end_b, end_c,
+    my_dec, got_dec, got_s, ret_s, inbound, sc_mine, sc_ctx, got_h, got_c,
+    sem_small, sem_x, sem_bc, sem_z, sem_out, sem_halo_s, sem_halo_r, sem_a, sem_s, sem_r,
 ):
     n_ctx, n_head, rows_all, heads, split = dims
     blocks = rows_all // Q
@@ -79,7 +86,7 @@
     many = n_ctx > 1
     me = lax.axis_index("ctx")
     me_head = lax.axis_index("head")
-    plane, lane_y = me // 4, me % 4
+    my_side, my_tile = me // 16, lax.rem(me // 2, TILES)
 
     load_small = [
         pltpu.make_async_copy(source, target, sem_small.at[i])
@@ -173,9 +180,18 @@
 
     sel_row, sel_head = iota((2 * heads, heads * 64), 0), iota((2 * heads, heads * 64), 1) // 64
     sel[...] = jnp.where((sel_row == sel_head) | (sel_row == sel_head + heads), 1.0, 0.0).astype(BF16)
-    keep_col = jnp.concatenate([1.0 - first, jnp.zeros((LANES - TABLE, LANES), F32)], axis=0).T
-    for k in range(blocks + 1):
-        keep[k * Q : (k + 1) * Q, :] = jnp.broadcast_to(keep_col[:, k : k + 1], (Q, LANES))
+    later = 1.0 - first
+    shifted = []
+    for lag in (1, 2):
+        here_l = pltpu.roll(later, lag, 1)
+        over = jnp.concatenate([here_l[:1], here_l[:-1]], axis=0)
+        shifted.append(jnp.where(iota((TABLE, LANES), 1) < lag, over, here_l))
+    stay2 = later * shifted[0]
+    stay3 = stay2 * shifted[1]
+    keep_col = jnp.concatenate([later, stay2, stay3, jnp.zeros((LANES - 3 * TABLE, LANES), F32)], axis=0).T
+    for k in range(blocks):
+        for j, m in enumerate((keep, keep2, keep3)):
+            m[k * Q : (k + 1) * Q, :] = jnp.broadcast_to(keep_col[:, j * TABLE + k + 1 : j * TABLE + k + 2], (Q, LANES))
 
     load_bc.wait()
     bc_taps = [conv_bc[lag] * 0.5 for lag in range(4)]
@@ -184,18 +200,9 @@
         prev = hbc[:, at : at + LANES] if k == 0 else bcs[k * Q - HALO : k * Q, at : at + LANES]
         half = half_conv(
             bcs[k * Q : (k + 1) * Q, at : at + LANES], prev,
-            [tap[:, at : at + LANES] for tap in bc_taps], keep[(k + 1) * Q - 8 : (k + 2) * Q, :],
+            [tap[:, at : at + LANES] for tap in bc_taps], [m[k * Q : (k + 1) * Q, :] for m in (keep, keep2, keep3)], buf, k % 6,
         )
         return twice_silu_half(half)
-
-    if many:
-        dec_all = jnp.exp2(by_pair(2 * blocks))
-        part_row = iota((16, LANES), 0)
-        for p in range(pairs):
-            hi, mid, low = (v.astype(F32) for v in three(dec_all[p : p + 1]))
-            tile = jnp.where(part_row == 0, hi, jnp.where(part_row == 1, mid, jnp.where(part_row == 2, low, 0.0)))
-            for part in range(4):
-                sbuf[p, part, PART:, :] = tile.astype(BF16)
 
     for k in range(1, blocks):
         btr[k] = conv_bc_block(k, 0).T.astype(BF16)
@@ -215,6 +222,21 @@
         )
         halo_x.start()
         halo_bc.start()
+        dec_all = jnp.exp2(by_pair(2 * blocks))
+        for p in range(4):
+            my_dec[p] = jnp.concatenate([dec_all[p : p + 1], dec_all[p + 4 : p + 5]], axis=0)
+
+        def send_dec(i, _):
+            other = lax.rem(me + i, n_ctx)
+            pltpu.make_async_remote_copy(
+                src_ref=my_dec.at[2 * lax.rem(other, 2) + other // 16], dst_ref=got_dec.at[me],
+                send_sem=sem_s.at[4], recv_sem=sem_r.at[4],
+                device_id={"ctx": other}, device_id_type=MESH,
+            ).start()
+            return 0
+
+        lax.fori_loop(1, n_ctx, send_dec, 0)
+        got_dec[me] = my_dec[2 * lax.rem(me, 2) + my_side]
     else:
         hx[...] = jnp.zeros_like(hx)
         hbc[...] = jnp.zeros_like(hbc)
@@ -222,62 +244,107 @@
     for copy in load_x:
         copy.wait()
 
+    def quad_of(i):
+        at = pl.multiple_of(i * QW, QW)
+        return i, at, [conv_x[lag : lag + 1, pl.ds(at, QW)] * 0.5 for lag in range(4)]
+
+    def weighed_block(quad, k):
+        q, at, taps = quad
+        prev = hx[:, pl.ds(at, QW)] if k == 0 else xq[q, k * Q - HALO : k * Q, :]
+        half = half_conv(xq[q, k * Q : (k + 1) * Q, :], prev, taps, [m[k * Q : (k + 1) * Q, :] for m in (keep, keep2, keep3)], buf, k % 6)
+        act = twice_silu_half(half)
+        xc[q, k * Q : (k + 1) * Q, :] = act.astype(BF16)
+        return (act * dot_t(whl[k], sel[:, pl.ds(at, QW)])).astype(BF16)
+
+    def by_quad(ref, k, q):
+        return jnp.concatenate([ref[k, pl.ds(2 * q, 1), :], ref[k, pl.ds(2 * q + 1, 1), :]], axis=1)
+
+    def first_block(i, _):
+        quad = quad_of(i)
+        q = quad[0]
+        block0 = dot(btr[0], weighed_block(quad, 0))
+        fresh[q] = block0
+        held = held_all[q] + block0 * by_quad(dec_one, blocks, q)
+        if many:
+            for u in range(2 * TILES):
+                side, tile = u // TILES, u % TILES
+                sbuf[q * 2 * TILES + u] = held[
+                    tile * PART : (tile + 1) * PART, side * LANES : (side + 1) * LANES
+                ].astype(BF16)
+            slot = q // 2
+
+            def send_state(u, _):
+                owner = 2 * u + lax.rem(q, 2)
+
+                @pl.when(owner != me)
+                def _():
+                    pltpu.make_async_remote_copy(
+                        src_ref=sbuf.at[q * 2 * TILES + u], dst_ref=got_s.at[slot * n_ctx + me],
+                        send_sem=sem_s.at[0], recv_sem=sem_a.at[slot],
+                        device_id={"ctx": owner}, device_id_type=MESH,
+                    ).start()
+
+                @pl.when(owner == me)
+                def _():
+                    got_s[slot * n_ctx + me] = sbuf[q * 2 * TILES + u]
+
+                return 0
+
+            lax.fori_loop(0, 2 * TILES, send_state, 0)
+        return 0
+
     def one_quad(i, _):
-        q = lax.rem(plane // 2 + i, quads) if many else i
-        at = pl.multiple_of(q * QW, QW)
-        taps = [conv_x[lag : lag + 1, pl.ds(at, QW)] * 0.5 for lag in range(4)]
-        pick = sel[:, pl.ds(at, QW)]
-
-        def weighed_block(k):
-            prev = hx[:, pl.ds(at, QW)] if k == 0 else xq[q, k * Q - HALO : k * Q, :]
-            half = half_conv(xq[q, k * Q : (k + 1) * Q, :], prev, taps, keep[(k + 1) * Q - 8 : (k + 2) * Q, :])
-            act = twice_silu_half(half)
-            xc[q, k * Q : (k + 1) * Q, :] = act.astype(BF16)
-            return (act * dot_t(whl[k], pick)).astype(BF16)
-
-        def by_quad(ref, k):
-            return jnp.concatenate([ref[k, pl.ds(2 * q, 1), :], ref[k, pl.ds(2 * q + 1, 1), :]], axis=1)
-
-        held = dot(btr[1], weighed_block(1))
+        quad = quad_of(i)
+        q = quad[0]
+        held = dot(btr[1], weighed_block(quad, 1))
         for k in range(2, blocks):
-            weighed = weighed_block(k)
+            weighed = weighed_block(quad, k)
             sk[q, k] = held.astype(BF16)
-            held = held * by_quad(dec_blk, k) + dot(btr[k], weighed)
-
-        @pl.when(i == 0)
+            held = held * by_quad(dec_blk, k, q) + dot(btr[k], weighed)
+        held_all[q] = held
+
+        @pl.when(i == 1)
         def _():
             if many:
                 halo_x.wait()
                 halo_bc.wait()
             btr[0] = conv_bc_block(0, 0).T.astype(BF16)
 
-        block0 = dot(btr[0], weighed_block(0))
-        fresh[q] = block0
-        held = held + block0 * by_quad(dec_one, blocks)
-        if many:
-            for side in range(2):
-                p = 2 * q + side
-                for part in range(4):
-                    owner = p * 4 + part
-                    sbuf[p, part, :PART, :] = held[
-                        part * PART : (part + 1) * PART, side * LANES : (side + 1) * LANES
-                    ].astype(BF16)
-
-                    @pl.when(owner != me)
-                    def _():
-                        pltpu.make_async_remote_copy(
-                            src_ref=sbuf.at[p, part], dst_ref=got_s.at[me],
-                            send_sem=sem_s.at[0], recv_sem=sem_r.at[0],
-                            device_id={"ctx": owner}, device_id_type=MESH,
-                        ).start()
-
-                    @pl.when(owner == me)
-                    def _():
-                        got_s[me] = sbuf[p, part]
-
+        lax.fori_loop(jnp.where(i == 1, 0, i), jnp.where(i == 0, 0, i + 1), first_block, 0)
         return 0
 
     lax.fori_loop(0, quads, one_quad, 0)
+
+    def all_of(sem, like, count):
+        view = like.at[pl.ds(0, count)]
+        pltpu.make_async_copy(view, view, sem).wait()
+
+    def scan_part(slot):
+        all_of(sem_a.at[slot], got_s, n_ctx - 1)
+        base = slot * n_ctx
+
+        def lap(d, acc):
+            ret_s[base + d] = acc.astype(BF16)
+            return acc * got_dec[d, slot : slot + 1, :] + got_s[base + d].astype(F32)
+
+        lax.fori_loop(0, n_ctx, lap, jnp.zeros((PART, LANES), F32), unroll=True)
+        target = (4 * slot + 2 * lax.rem(me, 2) + my_side) * TILES + my_tile
+
+        def send_back(i, _):
+            d = lax.rem(me + i, n_ctx)
+            pltpu.make_async_remote_copy(
+                src_ref=ret_s.at[base + d], dst_ref=inbound.at[target],
+                send_sem=sem_s.at[1], recv_sem=sem_r.at[1],
+                device_id={"ctx": d}, device_id_type=MESH,
+            ).start()
+            return 0
+
+        lax.fori_loop(1, n_ctx, send_back, 0)
+        inbound[target] = ret_s[base + me]
+
+    if many:
+        all_of(sem_r.at[4], got_dec, n_ctx - 1)
+        scan_part(0)
 
     causal = iota((Q, Q), 0) >= iota((Q, Q), 1)
     for k in range(blocks):
@@ -330,31 +397,8 @@
 
     lax.fori_loop(0, split, one_block, 0)
 
-    def all_of(sem, like, count):
-        view = like.at[pl.ds(0, count)]
-        pltpu.make_async_copy(view, view, sem).wait()
-
-    if many:
-        all_of(sem_r.at[0], got_s, n_ctx - 1)
-
-        def lap(d, acc):
-            ret_s[d] = acc.astype(BF16)
-            dec = jnp.sum(got_s[d, PART:, :].astype(F32), axis=0, keepdims=True)
-            return acc * dec + got_s[d, :PART, :].astype(F32)
-
-        lax.fori_loop(0, n_ctx, lap, jnp.zeros((PART, LANES), F32), unroll=True)
-
-        def send_back(i, _):
-            other = lax.rem(me + i, n_ctx)
-            pltpu.make_async_remote_copy(
-                src_ref=ret_s.at[other], dst_ref=inbound.at[plane, lane_y],
-                send_sem=sem_s.at[1], recv_sem=sem_r.at[1],
-                device_id={"ctx": other}, device_id_type=MESH,
-            ).start()
-            return 0
-
-        lax.fori_loop(1, n_ctx, send_back, 0)
-        inbound[plane, lane_y] = ret_s[me]
+    if many:
+        scan_part(1)
 
     lax.fori_loop(split, blocks, one_block, 0)
 
@@ -368,11 +412,11 @@
             end_b[c : c + 1, q * QW : (q + 1) * QW] = part_b[q, pl.ds(spot, 1), :] * mine
 
     if many:
-        all_of(sem_r.at[1], ret_s, n_ctx - 1)
+        all_of(sem_r.at[1], inbound, 2 * n_ctx - 2)
     else:
         inbound[...] = jnp.zeros_like(inbound)
     for p in range(pairs):
-        sin[:, p * LANES : (p + 1) * LANES] = inbound[p].reshape(LANES, LANES)
+        sin[:, p * LANES : (p + 1) * LANES] = inbound[p * TILES : (p + 1) * TILES].reshape(LANES, LANES)
 
     last = end_a[...] + end_b[...] * dot(end_c[...].astype(BF16), sin[...])
     width = heads * 64
@@ -430,10 +474,11 @@
         got_c[me] = score_row
     lax.fori_loop(blocks // 2, blocks, finish, 0)
     if many:
-        all_of(sem_s.at[0], got_s, n_ctx - 1)
-        all_of(sem_s.at[1], ret_s, n_ctx - 1)
+        all_of(sem_s.at[0], got_s, 2 * n_ctx - 2)
+        all_of(sem_s.at[1], ret_s, 2 * n_ctx - 2)
         all_of(sem_s.at[2], got_h, n_head - 1)
         all_of(sem_s.at[3], got_c, n_ctx - 1)
+        all_of(sem_s.at[4], got_dec, n_ctx - 1)
         all_of(sem_r.at[3], got_c, n_ctx - 1)
         score_row = jnp.sum(got_c[...], axis=0)
     score_ref[...] = score_row[0, : score_ref.shape[0]]
@@ -463,7 +508,10 @@
         pltpu.VMEM((quads, rows, QW), BF16),
         pltpu.VMEM((HALO, width), BF16),
         pltpu.VMEM((HALO, 256), BF16),
-        pltpu.VMEM((rows + Q, LANES), F32),
+        pltpu.VMEM((rows, LANES), F32),
+        pltpu.VMEM((rows, LANES), F32),
+        pltpu.VMEM((rows, LANES), F32),
+        pltpu.VMEM((12, Q + 8, LANES), F32),
         pltpu.VMEM((blocks, Q, Q), F32),
         pltpu.VMEM((blocks, heads, LANES), F32),
         pltpu.VMEM((blocks, 2 * heads, LANES), BF16),
@@ -479,8 +527,9 @@
         pltpu.VMEM((blocks, Q, Q), BF16),
         pltpu.VMEM((quads, blocks, LANES, QW), BF16),
         pltpu.VMEM((quads, LANES, QW), F32),
+        pltpu.VMEM((quads, LANES, QW), F32),
         pltpu.VMEM((blocks + 1, pairs, LANES), F32),
-        pltpu.VMEM((pairs, 4, MSG, LANES), BF16),
+        pltpu.VMEM((pairs * LANES // PART, PART, LANES), BF16),
         pltpu.VMEM((quads, rows, QW), F32),
         pltpu.VMEM((quads, rows, QW), F32),
         pltpu.VMEM((rows, width), BF16),
@@ -488,14 +537,16 @@
         pltpu.VMEM((TABLE, width), F32),
         pltpu.VMEM((TABLE, width), F32),
         pltpu.VMEM((TABLE, LANES), F32),
-        pltpu.VMEM((n_ctx, MSG, LANES), BF16),
-        pltpu.VMEM((n_ctx, PART, LANES), BF16),
-        pltpu.VMEM((pairs, 4, PART, LANES), BF16),
+        pltpu.VMEM((4, 2, LANES), F32),
+        pltpu.VMEM((n_ctx, 2, LANES), F32),
+        pltpu.VMEM((2 * n_ctx, PART, LANES), BF16),
+        pltpu.VMEM((2 * n_ctx, PART, LANES), BF16),
+        pltpu.VMEM((pairs * LANES // PART, PART, LANES), BF16),
         pltpu.VMEM((1, 1, LANES), F32),
         pltpu.VMEM((1, 1, LANES), F32),
         pltpu.VMEM((n_head, 1, LANES), F32),
         pltpu.VMEM((n_ctx, 1, LANES), F32),
-        dma((9,)), dma((quads,)), dma, dma((quads,)), dma, dma((2,)), dma((2,)), dma((4,)), dma((4,)),
+        dma((9,)), dma((quads,)), dma, dma((quads,)), dma, dma((2,)), dma((2,)), dma((2,)), dma((5,)), dma((5,)),
     ]
     params = dict(vmem_limit_bytes=50 * 1024 * 1024)
     if n_ctx > 1:

time: 51.4 us -> 47.6 us (0.926)
  Pallas kernels: 48.5 us -> 44.7 us
    pallas_call x1, Pallas kernels: 48.5 us -> 44.7 us  [local(): pl.pallas_call(functools.partial(kernel, (n_ctx, n_head, rows, heads, spl...]
where the time goes in v3:
time: 47.6 us
  Pallas kernels  44.7 us (94%)
  local copies, waits for them, and re-layouts  2.18 us (5%)
  between operations  0.64 us (1%)
    pallas_call x1, Pallas kernels, local(): pl.pallas_call(functools.partial(kernel, (n_ctx, n_head, rows, heads, spl...  44.7 us
    unnamed x2, local copies, waits for them, and re-layouts  2.18 us

profile of v3, /device:TPU:1, one launch (start us, length us, event | category | flops | bytes accessed | tf_op | source)
XLA Modules:
  0.0 47.6 jit_solution(14382580551259639731)
XLA Ops:
  0.6 44.7 %shard_map.131 = (bf16[1536,1024]{1,0:T(8,128)(2,1)S(1)}, f32[16]{0:T(128)S(1)}) custom-call(s32[16]{0:T(128)} %lengths_hbm.1, f32[16]{0:T(128)} %bias_hbm.1, f32[16]{0:T(128)} %a_log_hbm.1, f32[16]{0:T(128)} %d_skip_hbm.1, f32[16,1536]{1,0:T(8,128)} %bitcast.3, f32[4,1024]{1,0:T(4,128)} %conv_x_hbm.1, f32[4,1,256]{2,1,0:T(1,128)} %conv_bc_hbm.1, ...), custom_call_target="tpu_custom_call" | custom-call | tf_op jit(solution)/shard_map/pallas_call | solution.py:555
  45.4 1.7 %copy.16 = bf16[1536,1024]{1,0:T(8,128)(2,1)} copy(bf16[1536,1024]{1,0:T(8,128)(2,1)S(1)} %get-tuple-element.4) | data formatting | bytes 6291456
  47.0 0.5 %copy.17 = f32[16]{0:T(128)} copy(f32[16]{0:T(128)S(1)} %get-tuple-element.5) | data formatting | bytes 128

commit v4 on v3

--- a/solution.py
+++ b/solution.py
@@ -235,7 +235,7 @@
             ).start()
             return 0
 
-        lax.fori_loop(1, n_ctx, send_dec, 0)
+        lax.fori_loop(1, n_ctx, send_dec, 0, unroll=True)
         got_dec[me] = my_dec[2 * lax.rem(me, 2) + my_side]
     else:
         hx[...] = jnp.zeros_like(hx)
@@ -284,13 +284,14 @@
                         device_id={"ctx": owner}, device_id_type=MESH,
                     ).start()
 
-                @pl.when(owner == me)
-                def _():
-                    got_s[slot * n_ctx + me] = sbuf[q * 2 * TILES + u]
-
                 return 0
 
-            lax.fori_loop(0, 2 * TILES, send_state, 0)
+            lax.fori_loop(0, 2 * TILES, send_state, 0, unroll=True)
+
+            @pl.when(lax.rem(q, 2) == lax.rem(me, 2))
+            def _():
+                got_s[slot * n_ctx + me] = sbuf[q * 2 * TILES + me // 2]
+
         return 0
 
     def one_quad(i, _):
@@ -339,7 +340,7 @@
             ).start()
             return 0
 
-        lax.fori_loop(1, n_ctx, send_back, 0)
+        lax.fori_loop(1, n_ctx, send_back, 0, unroll=True)
         inbound[target] = ret_s[base + me]
 
     if many:
@@ -436,7 +437,7 @@
             ).start()
             return 0
 
-        lax.fori_loop(1, n_head, to_head, 0)
+        lax.fori_loop(1, n_head, to_head, 0, unroll=True)
         got_h[me_head] = score_row
 
     def finish(k, _):
@@ -470,7 +471,7 @@
             ).start()
             return 0
 
-        lax.fori_loop(1, n_ctx, to_ctx, 0)
+        lax.fori_loop(1, n_ctx, to_ctx, 0, unroll=True)
         got_c[me] = score_row
     lax.fori_loop(blocks // 2, blocks, finish, 0)
     if many:
@@ -551,7 +552,7 @@
     params = dict(vmem_limit_bytes=50 * 1024 * 1024)
     if n_ctx > 1:
         params.update(collective_id=0, has_side_effects=True)
-    split = min(3, blocks)
+    split = min(5, blocks)
     return pl.pallas_call(
         functools.partial(kernel, (n_ctx, n_head, rows, heads, split)),
         out_shape=(jax.ShapeDtypeStruct((rows, width), BF16), jax.ShapeDtypeStruct(lengths.shape, F32)),

time: 47.6 us -> 46.1 us (0.968)
  Pallas kernels: 44.7 us -> 43.2 us
    pallas_call x1, Pallas kernels: 44.7 us -> 43.2 us  [local(): pl.pallas_call(functools.partial(kernel, (n_ctx, n_head, rows, heads, spl...]
where the time goes in v4:
time: 46.1 us; the launch traced here: 46 us
  Pallas kernels  43.2 us (94%)
  local copies, waits for them, and re-layouts  2.18 us (5%)
  between operations  0.64 us (1%)
    pallas_call x1, Pallas kernels, local(): pl.pallas_call(functools.partial(kernel, (n_ctx, n_head, rows, heads, spl...  43.2 us
    unnamed x2, local copies, waits for them, and re-layouts  2.18 us

profile of v4, /device:TPU:1, one launch (start us, length us, event | category | flops | bytes accessed | tf_op | source)
XLA Modules:
  0.0 46.0 jit_solution(15607898640425723960)
XLA Ops:
  0.6 43.2 %shard_map.131 = (bf16[1536,1024]{1,0:T(8,128)(2,1)S(1)}, f32[16]{0:T(128)S(1)}) custom-call(s32[16]{0:T(128)} %lengths_hbm.1, f32[16]{0:T(128)} %bias_hbm.1, f32[16]{0:T(128)} %a_log_hbm.1, f32[16]{0:T(128)} %d_skip_hbm.1, f32[16,1536]{1,0:T(8,128)} %bitcast.3, f32[4,1024]{1,0:T(4,128)} %conv_x_hbm.1, f32[4,1,256]{2,1,0:T(1,128)} %conv_bc_hbm.1, ...), custom_call_target="tpu_custom_call" | custom-call | tf_op jit(solution)/shard_map/pallas_call | solution.py:556
  43.8 1.7 %copy.16 = bf16[1536,1024]{1,0:T(8,128)(2,1)} copy(bf16[1536,1024]{1,0:T(8,128)(2,1)S(1)} %get-tuple-element.4) | data formatting | bytes 6291456
  45.5 0.5 %copy.17 = f32[16]{0:T(128)} copy(f32[16]{0:T(128)S(1)} %get-tuple-element.5) | data formatting | bytes 128

commit v5 on v4

--- a/solution.py
+++ b/solution.py
@@ -252,9 +252,9 @@
         q, at, taps = quad
         prev = hx[:, pl.ds(at, QW)] if k == 0 else xq[q, k * Q - HALO : k * Q, :]
         half = half_conv(xq[q, k * Q : (k + 1) * Q, :], prev, taps, [m[k * Q : (k + 1) * Q, :] for m in (keep, keep2, keep3)], buf, k % 6)
-        act = twice_silu_half(half)
-        xc[q, k * Q : (k + 1) * Q, :] = act.astype(BF16)
-        return (act * dot_t(whl[k], sel[:, pl.ds(at, QW)])).astype(BF16)
+        act = twice_silu_half(half).astype(BF16)
+        xc[q, k * Q : (k + 1) * Q, :] = act
+        return act * dot_t(whl[k], sel[:, pl.ds(at, QW)]).astype(BF16)
 
     def by_quad(ref, k, q):
         return jnp.concatenate([ref[k, pl.ds(2 * q, 1), :], ref[k, pl.ds(2 * q + 1, 1), :]], axis=1)

time: 46.1 us -> 46.1 us (level)
  no operation moved by 1% of the time
where the time goes in v5:
time: 46.1 us; the launch traced here: 46 us
  Pallas kernels  43.2 us (94%)
  local copies, waits for them, and re-layouts  2.18 us (5%)
  between operations  0.64 us (1%)
    pallas_call x1, Pallas kernels, local(): pl.pallas_call(functools.partial(kernel, (n_ctx, n_head, rows, heads, spl...  43.2 us
    unnamed x2, local copies, waits for them, and re-layouts  2.18 us

profile of v5, /device:TPU:1, one launch (start us, length us, event | category | flops | bytes accessed | tf_op | source)
XLA Modules:
  0.0 46.0 jit_solution(7218703253004565713)
XLA Ops:
  0.6 43.2 %shard_map.131 = (bf16[1536,1024]{1,0:T(8,128)(2,1)S(1)}, f32[16]{0:T(128)S(1)}) custom-call(s32[16]{0:T(128)} %lengths_hbm.1, f32[16]{0:T(128)} %bias_hbm.1, f32[16]{0:T(128)} %a_log_hbm.1, f32[16]{0:T(128)} %d_skip_hbm.1, f32[16,1536]{1,0:T(8,128)} %bitcast.3, f32[4,1024]{1,0:T(4,128)} %conv_x_hbm.1, f32[4,1,256]{2,1,0:T(1,128)} %conv_bc_hbm.1, ...), custom_call_target="tpu_custom_call" | custom-call | tf_op jit(solution)/shard_map/pallas_call | solution.py:556
  43.8 1.7 %copy.16 = bf16[1536,1024]{1,0:T(8,128)(2,1)} copy(bf16[1536,1024]{1,0:T(8,128)(2,1)S(1)} %get-tuple-element.4) | data formatting | bytes 6291456
  45.5 0.5 %copy.17 = f32[16]{0:T(128)} copy(f32[16]{0:T(128)S(1)} %get-tuple-element.5) | data formatting | bytes 128
